TPU v7x, 32 devices: a whole 2x2x4 slice. The times are simulated.
32 devices in a mesh: elem: 8 (over z, y), mode: 4 (over x, core).
Axes of the slice: x: 2, y: 2, z: 4, core: 2. Of those that a mesh axis runs over, the one named last changes fastest.
Arguments:
- modal_history: float32 [4096, 512], P('elem', 'mode'), may hold values from -6 to 6
- stress_modes: float32 [512, 384], P('mode', 'elem'), may hold values from -0.375 to 0.375
Outputs:
- stress_spectrum: float32 [384, 2, 2048], P(('elem', 'mode'))
All inputs are finite; a program needn't handle non-finite values.
Results may differ from a plain program's by a relative error of at most 0.00007.
Values sent between devices are 32-bit elements; how exact they have to be, the bound alone decides.
A program may use at most 64 MiB of HBM per device.

v0:
```python
import math

import jax
import jax.numpy as jnp
from jax import lax
from jax.sharding import PartitionSpec as P

highest = lax.Precision.HIGHEST


def spectra(signal):
    columns = signal.shape[0]
    radix = 64
    halved = radix // 2
    blocked = signal.reshape(columns, radix, radix)
    counter = jnp.arange(radix, dtype=jnp.int32)
    products = counter[:, None] * counter[None, :]
    small_angle = (products % radix).astype(jnp.float32) * (2.0 * math.pi / radix)
    cosine_small = jnp.cos(small_angle)
    sine_small = jnp.sin(small_angle)
    twist_angle = (products % (radix * radix)).astype(jnp.float32) * (
        2.0 * math.pi / (radix * radix)
    )
    twist_cos = jnp.cos(twist_angle)
    twist_sin = jnp.sin(twist_angle)
    first_real = jnp.einsum("cab,ak->cbk", blocked, cosine_small, precision=highest)
    first_imag = -jnp.einsum("cab,ak->cbk", blocked, sine_small, precision=highest)
    turned_real = first_real * twist_cos + first_imag * twist_sin
    turned_imag = first_imag * twist_cos - first_real * twist_sin
    cosine_half = cosine_small[:, :halved]
    sine_half = sine_small[:, :halved]
    final_real = jnp.einsum(
        "cbk,bj->cjk", turned_real, cosine_half, precision=highest
    ) + jnp.einsum("cbk,bj->cjk", turned_imag, sine_half, precision=highest)
    final_imag = jnp.einsum(
        "cbk,bj->cjk", turned_imag, cosine_half, precision=highest
    ) - jnp.einsum("cbk,bj->cjk", turned_real, sine_half, precision=highest)
    stacked = jnp.stack([final_real, final_imag], axis=1) * (1.0 / radix)
    return stacked.reshape(columns, 2, halved * radix)


def per_device(modal_history, stress_modes):
    elem_count = lax.axis_size("elem")
    mode_count = lax.axis_size("mode")
    local_steps = modal_history.shape[0]
    partial_value = jnp.einsum(
        "mp,tm->pt",
        lax.all_gather(stress_modes, "elem", axis=1, tiled=True),
        modal_history,
        precision=highest,
        preferred_element_type=jnp.float32,
    )
    owned_width = partial_value.shape[0] // (elem_count * mode_count)
    reordered = partial_value.reshape(elem_count, mode_count, owned_width, local_steps)
    reordered = reordered.transpose(1, 0, 2, 3).reshape(
        mode_count * elem_count * owned_width, local_steps
    )
    summed = lax.psum_scatter(reordered, "mode", scatter_dimension=0, tiled=True)
    stress = lax.all_to_all(summed, "elem", split_axis=0, concat_axis=1, tiled=True)
    return spectra(stress)


def solution(mesh):
    placed = (P("elem", "mode"), P("mode", "elem"))
    return jax.shard_map(
        per_device,
        mesh=mesh,
        in_specs=placed,
        out_specs=P(("elem", "mode"), None, None),
        check_vma=False,
    )
```

profile of v0, /device:TPU:0, one launch (start us, length us, event | category | flops | bytes accessed | tf_op | source)
XLA Modules:
  0.0 93.0 jit_solution(17106612503640794953)
XLA Ops:
  6.5 0.0 copy-start
  6.5 0.0 reduce-scatter.2.cloned.1.call-start
  6.5 32.7 %all_gather.3 = f32[128,384]{0,1:T(8,128)S(1)} all-gather(f32[128,48]{0,1:T(8,128)} %param.3), channel_id=1, replica_groups=mesh['elem'=8,'mode'=4] {'elem'}, dimensions={1}, use_global_device_ids=true | all-gather | bytes 221184 | tf_op jit(solution)/shard_map/all_gather | solution.py:48
  39.3 0.0 copy-done
  39.3 0.8 fusion.32
  40.1 0.1 reshape.54
  40.2 0.1 copy.9
  40.3 1.0 %reshape.55 = f32[384,512]{1,0:T(8,128)} reshape(f32[4,8,12,512]{3,2,1,0:T(8,128)S(1)} %copy.9) | data formatting | bytes 1572864 | tf_op jit(solution)/shard_map/reshape | solution.py:55
  41.3 0.0 reduce-scatter.2.cloned.1.call-update
  41.3 24.4 %reduce-scatter.2.cloned.1.call-done = f32[96,512]{1,0:T(8,128)} async-done(((f32[384,512]{1,0:T(8,128)}), f32[96,512]{1,0:T(8,128)}) %reduce-scatter.2.cloned.1.call-update) | async-done | bytes 196624 | tf_op jit(solution)/shard_map/reduce_scatter | solution.py:58
  65.6 1.6 %all_to_all.12 = f32[8,12,512]{2,1,0:T(8,128)} reshape(f32[96,512]{1,0:T(8,128)} %reduce-scatter.2.cloned.1.call-done) | data formatting | bytes 393216 | tf_op jit(solution)/shard_map/all_to_all | solution.py:59
  67.3 5.5 %all-to-all-start = ((f32[8,12,512]{2,1,0:T(8,128)}), f32[8,12,512]{2,1,0:T(8,128)S(1)}, u32[]{:S(2)}, u32[]{:S(2)}) async-start(f32[8,12,512]{2,1,0:T(8,128)} %all_to_all.12), calls=%async_computation.1 | async-start | bytes 524288 | tf_op jit(solution)/shard_map/all_to_all | solution.py:59
  72.8 0.1 fusion.19
  73.0 0.1 copy.13
  73.0 0.2 fusion.18
  73.2 0.1 copy.16
  73.3 0.2 fusion.21
  73.4 0.1 fusion.20
  73.6 8.2 %all-to-all-done = f32[8,12,512]{2,1,0:T(8,128)S(1)} async-done(((f32[8,12,512]{2,1,0:T(8,128)}), f32[8,12,512]{2,1,0:T(8,128)S(1)}, u32[]{:S(2)}, u32[]{:S(2)}) %all-to-all-start) | async-done | bytes 196640 | tf_op jit(solution)/shard_map/all_to_all | solution.py:59
  81.7 0.1 copy.10
  81.8 0.1 reshape.56
  82.0 0.8 convolution_negate_fusion
  82.8 0.8 fusion.9
  83.6 0.4 fusion.2
  84.0 0.4 fusion.3
  84.3 0.4 fusion.1
  84.7 0.1 stack.9
  84.8 0.4 fusion
  85.2 0.1 stack.10
  85.3 0.8 copy.17
  (1 shorter events, 0.0 us)
Async XLA Ops:
  6.5 32.8 %copy-start = (f32[512,128]{1,0:T(8,128)S(1)}, f32[512,128]{1,0:T(8,128)}, u32[]{:S(2)}) copy-start(f32[512,128]{1,0:T(8,128)} %param.2) | copy-start | bytes 786436
  6.5 59.1 %reduce-scatter.2.cloned.1.call-start = ((), (), s32[]{:S(2)}) async-start(), calls=%async_computation.2 | async-start | bytes 983040 | tf_op jit(solution)/shard_map/reduce_scatter | solution.py:58
  67.3 14.4 %all-to-all-start = ((f32[8,12,512]{2,1,0:T(8,128)}), f32[8,12,512]{2,1,0:T(8,128)S(1)}, u32[]{:S(2)}, u32[]{:S(2)}) async-start(f32[8,12,512]{2,1,0:T(8,128)} %all_to_all.12), calls=%async_computation.1 | async-start | bytes 524288 | tf_op jit(solution)/shard_map/all_to_all | solution.py:59
Sparse Core Ops, SparseCore 0:
  41.4 24.1 reduce-scatter.1
where the time goes:
time: 93.2 us; the launch traced here: 93 us
  blocking collectives  32.7 us (35%)
  waiting for transfers between devices  32.5 us (35%)
  between operations  13.5 us (14%)
  starting transfers between devices  5.52 us (6%)
  local copies, waits for them, and re-layouts  4.24 us (5%)
  matrix products  3.84 us (4%)
    all_gather x1, blocking collectives, per_device(): lax.all_gather(stress_modes, 'elem', axis=1, tiled=True)  32.7 us
    reduce_scatter x1, waiting for transfers between devices, per_device(): lax.psum_scatter(reordered, 'mode', scatter_dimension=0, tiled=True)  24.4 us
    all_to_all x1, waiting for transfers between devices, per_device(): lax.all_to_all(summed, 'elem', split_axis=0, concat_axis=1, tiled=True)  8.17 us
    all_to_all x1, starting transfers between devices, per_device(): lax.all_to_all(summed, 'elem', split_axis=0, concat_axis=1, tiled=True)  5.52 us
  transfers between devices with their start and end apart: 2, of which 2 were waited for; matrix products, arithmetic and copies ran while one was open for 1% of the time, Pallas kernels for 0%

commit v1 on v0

--- a/solution.py
+++ b/solution.py
@@ -1,11 +1,21 @@
+import functools
 import math
 
 import jax
 import jax.numpy as jnp
+import ml_dtypes
+import numpy as np
 from jax import lax
+from jax.experimental import pallas as pl
+from jax.experimental.pallas import tpu as pltpu
 from jax.sharding import PartitionSpec as P
 
 highest = lax.Precision.HIGHEST
+MESH = pl.DeviceIdType.MESH
+f32, bf16 = jnp.float32, jnp.bfloat16
+
+RADIX = 128
+REST = 32
 
 
 def spectra(signal):
@@ -39,7 +49,7 @@
     return stacked.reshape(columns, 2, halved * radix)
 
 
-def per_device(modal_history, stress_modes):
+def plain(modal_history, stress_modes):
     elem_count = lax.axis_size("elem")
     mode_count = lax.axis_size("mode")
     local_steps = modal_history.shape[0]
@@ -60,6 +70,278 @@
     return spectra(stress)
 
 
+def split_np(x):
+    hi = x.astype(np.float32).astype(ml_dtypes.bfloat16)
+    lo = (x - hi.astype(np.float64)).astype(np.float32).astype(ml_dtypes.bfloat16)
+    return hi, lo
+
+
+def tables(steps):
+    two_pi = 2.0 * np.pi
+    a = np.arange(RADIX)
+    ang = two_pi * ((a[:, None] * a[None, :]) % RADIX) / RADIX
+    first = np.concatenate([np.cos(ang), -np.sin(ang)], axis=1)
+    first_hi, first_lo = split_np(first)
+    row = np.arange(REST)
+    b = (row % 4) * 8 + row // 4
+    twist = two_pi * ((b[:, None] * a[None, :]) % steps) / steps
+    k2 = np.arange(REST // 2)
+    last = two_pi * ((k2[:, None] * b[None, :]) % REST) / REST
+    real = np.concatenate([np.cos(last), np.sin(last)], axis=1)
+    imag = np.concatenate([-np.sin(last), np.cos(last)], axis=1)
+    second = np.stack([real, imag], axis=1).reshape(REST, 2 * REST) / math.sqrt(steps)
+    second_hi, second_lo = split_np(second)
+    second_all = np.concatenate([second_hi, second_hi, second_lo], axis=1)
+    twist_all = np.stack([np.cos(twist), np.sin(twist)]).astype(np.float32)
+    return first_hi, first_lo, twist_all, second_all
+
+
+def split(x):
+    hi = x.astype(bf16)
+    lo = (x - hi.astype(f32)).astype(bf16)
+    return hi, lo
+
+
+def nt(a, b):
+    return lax.dot_general(
+        a, b, (((1,), (1,)), ((), ())), preferred_element_type=f32
+    )
+
+
+def nn(a, b):
+    return jnp.dot(a, b, preferred_element_type=f32)
+
+
+def fused(
+    elems, modes, width,
+    hist, shape_ref, first_hi, first_lo, twist, second,
+    out,
+    hbuf, s_send, s_recv, gathered, s_all, outbox, inbox, turned,
+    own_sem, hs_sem, hr_sem, s1s_sem, s1r_sem, s2s_sem, s2r_sem, as_sem, ar_sem,
+):
+    chunks = 2
+    e = lax.axis_index("elem")
+    m = lax.axis_index("mode")
+    sibling = m + 1 - 2 * (m % 2)
+    across = (m + 2) % modes
+    diagonal = (modes - 1) - m
+
+    barrier = pltpu.get_barrier_semaphore()
+    for peer in (sibling, across, diagonal):
+        pl.semaphore_signal(barrier, inc=1, device_id=(e, peer), device_id_type=MESH)
+    for d in range(1, elems):
+        pl.semaphore_signal(
+            barrier, inc=1, device_id=((e + d) % elems, m), device_id_type=MESH
+        )
+
+    own = [
+        pltpu.make_async_copy(hist.at[:, c], hbuf.at[m, c], own_sem.at[c])
+        for c in range(chunks)
+    ]
+    for copy in own:
+        copy.start()
+
+    modes_t = shape_ref[...].T
+    for p in range(modes):
+        s_send[p, :width, :] = modes_t[p * width : (p + 1) * width, :]
+    s_recv[m, :width, :] = s_send[m, :width, :]
+    s_all[...] = jnp.zeros_like(s_all)
+
+    pl.semaphore_wait(barrier, modes - 1 + elems - 1)
+
+    first_copies = []
+    for i, peer in enumerate((across, diagonal, sibling)):
+        first_copies.append((
+            pltpu.make_async_remote_copy(
+                s_send.at[peer], s_recv.at[m], s1s_sem.at[i], s1r_sem.at[i],
+                device_id=(e, peer), device_id_type=MESH,
+            ),
+            pltpu.make_async_remote_copy(
+                s_send.at[peer], s_recv.at[peer], s1s_sem.at[i], s1r_sem.at[i],
+                device_id=(e, peer), device_id_type=MESH,
+            ),
+        ))
+    for copy, _ in first_copies:
+        copy.start()
+
+    def history_copy(kind, c, origin, peer):
+        src = hist.at[:, c] if kind < 2 else hbuf.at[origin, c]
+        return pltpu.make_async_remote_copy(
+            src, hbuf.at[origin, c], hs_sem.at[kind, c], hr_sem.at[kind, c],
+            device_id=(e, peer), device_id_type=MESH,
+        )
+
+    to_across = [history_copy(0, c, m, across) for c in range(chunks)]
+    to_sibling = [history_copy(1, c, m, sibling) for c in range(chunks)]
+    forward = [history_copy(2, c, across, sibling) for c in range(chunks)]
+    from_across = [history_copy(0, c, across, across) for c in range(chunks)]
+    from_sibling = [history_copy(1, c, sibling, sibling) for c in range(chunks)]
+    from_forward = [history_copy(2, c, diagonal, sibling) for c in range(chunks)]
+    for c in range(chunks):
+        to_across[c].start()
+        to_sibling[c].start()
+
+    for _, landed in first_copies:
+        landed.wait_recv()
+    for p in range(modes):
+        gathered[e, p * width : (p + 1) * width, :] = s_recv[p, :width, :]
+
+    order = sorted(range(1, elems), key=lambda d: -min(d, elems - d))
+    second_copies = []
+    for d in order:
+        peer, source = (e + d) % elems, (e + elems - d) % elems
+        copy = pltpu.make_async_remote_copy(
+            gathered.at[e], gathered.at[e], s2s_sem.at[d], s2r_sem.at[d],
+            device_id=(peer, m), device_id_type=MESH,
+        )
+        landed = pltpu.make_async_remote_copy(
+            gathered.at[source], gathered.at[source], s2s_sem.at[d], s2r_sem.at[d],
+            device_id=(peer, m), device_id_type=MESH,
+        )
+        copy.start()
+        second_copies.append((copy, landed))
+
+    for c in range(chunks):
+        from_across[c].wait_recv()
+        forward[c].start()
+
+    for _, landed in second_copies:
+        landed.wait_recv()
+    for owner in range(elems):
+        for p in range(modes):
+            s_all[owner * 16 : owner * 16 + width, p * 128 : (p + 1) * 128] = (
+                gathered[owner, p * width : (p + 1) * width, :]
+            )
+    s_hi, s_lo = split(s_all[...])
+    s_both = jnp.concatenate([s_hi, s_lo], axis=0)
+    rows = s_hi.shape[0]
+
+    last_copies = []
+    for c in range(chunks):
+        own[c].wait()
+        from_sibling[c].wait_recv()
+        from_forward[c].wait_recv()
+        pieces = []
+        for p in range(modes):
+            flat = hbuf.at[p, c].reshape(256, 128)
+            pieces.append(
+                jnp.concatenate(
+                    [flat[pl.ds(i, 16, stride=16), :] for i in range(16)], axis=0
+                )
+            )
+        h_hi, h_lo = split(jnp.concatenate(pieces, axis=1))
+        both = nt(s_both, h_hi)
+        stress = both[:rows] + (both[rows:] + nt(s_hi, h_lo))
+        for owner in range(elems):
+            for h in range(2):
+                outbox[owner, c, h * width : (h + 1) * width, :] = stress[
+                    owner * 16 : owner * 16 + width, h * 128 : (h + 1) * 128
+                ]
+        for d in order:
+            peer, source = (e + d) % elems, (e + elems - d) % elems
+            copy = pltpu.make_async_remote_copy(
+                outbox.at[peer, c], inbox.at[e, c], as_sem.at[d, c], ar_sem.at[d, c],
+                device_id=(peer, m), device_id_type=MESH,
+            )
+            landed = pltpu.make_async_remote_copy(
+                outbox.at[peer, c], inbox.at[source, c], as_sem.at[d, c],
+                ar_sem.at[d, c], device_id=(peer, m), device_id_type=MESH,
+            )
+            copy.start()
+            last_copies.append((copy, landed))
+        inbox[e, c] = outbox[e, c]
+
+    for _, landed in last_copies:
+        landed.wait_recv()
+
+    blocks = [
+        jnp.concatenate([inbox[i, 0], inbox[i, 1]], axis=0) for i in range(elems)
+    ]
+    group = lax.broadcasted_iota(jnp.int32, blocks[0].shape, 1) // 16
+    for step in (4, 2, 1):
+        low = (group // step) % 2 == 0
+        for i in range(elems):
+            if (i // step) % 2 == 0:
+                one, two = blocks[i], blocks[i + step]
+                blocks[i] = jnp.where(low, one, pltpu.roll(two, 16 * step, 1))
+                blocks[i + step] = jnp.where(
+                    low, pltpu.roll(one, 128 - 16 * step, 1), two
+                )
+    x_hi, x_lo = split(jnp.concatenate(blocks, axis=0))
+    w_hi, w_lo = first_hi[...], first_lo[...]
+    once = nn(x_hi, w_hi) + (nn(x_lo, w_hi) + nn(x_hi, w_lo))
+    turned[0] = once[:, :128]
+    turned[1] = once[:, 128:]
+
+    cos, sin = twist[0], twist[1]
+    real, imag = [], []
+    for col in range(width):
+        re = turned.at[0][pl.ds(col, REST, stride=width), :]
+        im = turned.at[1][pl.ds(col, REST, stride=width), :]
+        real.append(re * cos + im * sin)
+        imag.append(im * cos - re * sin)
+    z = jnp.concatenate(
+        [jnp.concatenate(real, axis=1), jnp.concatenate(imag, axis=1)], axis=0
+    )
+    z_hi, z_lo = split(z)
+    result = nn(second[...], jnp.concatenate([z_hi, z_lo, z_hi], axis=0))
+    for col in range(width):
+        out[col] = result[:, col * 128 : (col + 1) * 128]
+
+    for copy, _ in first_copies + second_copies + last_copies:
+        copy.wait_send()
+    for copy in to_across + to_sibling + forward:
+        copy.wait_send()
+
+
+def with_kernel(modal_history, stress_modes):
+    elems, modes = lax.axis_size("elem"), lax.axis_size("mode")
+    steps = modal_history.shape[0] * elems
+    width = stress_modes.shape[1] // modes
+    consts = [jnp.asarray(t) for t in tables(steps)]
+    hist = modal_history.reshape(16, 2, 16, 128)
+    vmem = pl.BlockSpec(memory_space=pltpu.VMEM)
+    dma = pltpu.SemaphoreType.DMA
+    result = pl.pallas_call(
+        functools.partial(fused, elems, modes, width),
+        out_shape=jax.ShapeDtypeStruct((width, REST, RADIX), f32),
+        in_specs=[pl.BlockSpec(memory_space=pl.ANY)] + [vmem] * 5,
+        out_specs=vmem,
+        scratch_shapes=[
+            pltpu.VMEM((modes, 2, 16, 16, 128), f32),
+            pltpu.VMEM((modes, 16, 128), f32),
+            pltpu.VMEM((modes, 16, 128), f32),
+            pltpu.VMEM((elems, modes * width, 128), f32),
+            pltpu.VMEM((elems * 16, modes * 128), f32),
+            pltpu.VMEM((elems, 2, 2 * width, 128), f32),
+            pltpu.VMEM((elems, 2, 2 * width, 128), f32),
+            pltpu.VMEM((2, REST * width, 128), f32),
+            dma((2,)),
+            dma((3, 2)), dma((3, 2)),
+            dma((3,)), dma((3,)),
+            dma((elems,)), dma((elems,)),
+            dma((elems, 2)), dma((elems, 2)),
+        ],
+        compiler_params=pltpu.CompilerParams(
+            collective_id=0, has_side_effects=True, vmem_limit_bytes=32 * 1024 * 1024
+        ),
+    )(hist, stress_modes, *consts)
+    ordered = result.reshape(width, REST // 2, 2, RADIX).transpose(0, 2, 1, 3)
+    return ordered.reshape(width, 2, REST // 2 * RADIX)
+
+
+def per_device(modal_history, stress_modes):
+    elems, modes = lax.axis_size("elem"), lax.axis_size("mode")
+    fits = (
+        elems == 8
+        and modes == 4
+        and modal_history.shape == (512, 128)
+        and stress_modes.shape == (128, 48)
+    )
+    body = with_kernel if fits else plain
+    return body(modal_history, stress_modes)
+
+
 def solution(mesh):
     placed = (P("elem", "mode"), P("mode", "elem"))
     return jax.shard_map(

time: 93.2 us -> 27.9 us (0.30)
  blocking collectives: 32.7 us -> 0 us
  waiting for transfers between devices: 32.5 us -> 0 us
  Pallas kernels: 0 us -> 23.4 us
  between operations: 13.5 us -> 0.04 us
  starting transfers between devices: 5.52 us -> 0 us
  matrix products: 3.84 us -> 0 us
    all_gather x1 -> x0, blocking collectives: 32.7 us -> none  [per_device(): lax.all_gather(stress_modes, 'elem', axis=1, tiled=True)]
    reduce_scatter x1 -> x0, waiting for transfers between devices: 24.4 us -> none  [per_device(): lax.psum_scatter(reordered, 'mode', scatter_dimension=0, tiled=True)]
    pallas_call x0 -> x1, Pallas kernels: none -> 23.4 us  [with_kernel(): pl.pallas_call(functools.partial(fused, elems, modes, width), out_shape=j...]
    all_to_all x1 -> x0, waiting for transfers between devices: 8.17 us -> none  [per_device(): lax.all_to_all(summed, 'elem', split_axis=0, concat_axis=1, tiled=True)]
    all_to_all x1 -> x0, starting transfers between devices: 5.52 us -> none  [per_device(): lax.all_to_all(summed, 'elem', split_axis=0, concat_axis=1, tiled=True)]
    unnamed x2 -> x12, local copies, waits for them, and re-layouts: 0.01 us -> 4.09 us
    dot_general x7 -> x0, matrix products: 3.84 us -> none  [the longest x1 0.81 us: spectra(): jnp.einsum('cab,ak->cbk', blocked, cosine_small, precision=highest)]
    all_to_all x2 -> x0, local copies, waits for them, and re-layouts: 1.76 us -> none  [per_device(): lax.all_to_all(summed, 'elem', split_axis=0, concat_axis=1, tiled=True)]
  transfers between devices with their start and end apart: 2 -> 0, of which waited for: 2 -> 0; matrix products, arithmetic and copies ran while one was open for 1% -> 0% of each run, Pallas kernels for 0% -> 0%
where the time goes in v1:
time: 27.9 us; the launch traced here: 27.6 us
  Pallas kernels  23.4 us (84%)
  local copies, waits for them, and re-layouts  4.09 us (15%)
    pallas_call x1, Pallas kernels, with_kernel(): pl.pallas_call(functools.partial(fused, elems, modes, width), out_shape=j...  23.4 us
    unnamed x12, local copies, waits for them, and re-layouts  4.09 us

profile of v1, /device:TPU:0, one launch (start us, length us, event | category | flops | bytes accessed | tf_op | source)
XLA Modules:
  0.0 27.6 jit_solution(14337023409214299586)
XLA Ops:
  0.0 0.0 copy-start.1
  0.0 0.0 copy-start.4
  0.0 0.9 %copy.7.shape_ref = f32[128,48]{1,0:T(8,128)S(1)} copy(f32[128,48]{0,1:T(8,128)} %param.7) | data formatting | bytes 49152 | tf_op args[1]
  0.9 0.0 copy-done.1
  0.9 0.0 copy-done.4
  0.9 0.0 copy-start
  0.9 0.9 %copy-done = f32[512,128]{1,0:T(8,128)S(1)} copy-done((f32[512,128]{1,0:T(8,128)S(1)}, f32[512,128]{1,0:T(8,128)}, u32[]{:S(2)}) %copy-start) | copy-done | bytes 262168
  1.8 0.0 copy-start.2
  1.8 0.8 %copy-done.2 = bf16[128,256]{1,0:T(8,128)(2,1)S(1)} copy-done((bf16[128,256]{1,0:T(8,128)(2,1)S(1)}, bf16[128,256]{1,0:T(8,128)(2,1)}, u32[]{:S(2)}) %copy-start.2) | copy-done | bytes 65560
  2.7 0.0 copy-start.3
  2.7 0.8 %copy-done.3 = f32[2,32,128]{2,1,0:T(8,128)S(1)} copy-done((f32[2,32,128]{2,1,0:T(8,128)S(1)}, f32[2,32,128]{2,1,0:T(8,128)}, u32[]{:S(2)}) %copy-start.3) | copy-done | bytes 32792
  3.4 23.4 %shard_map.64 = f32[12,32,128]{2,1,0:T(8,128)S(1)} custom-call(f32[16,2,16,128]{3,2,1,0:T(8,128)S(1)} %bitcast.7, f32[128,48]{1,0:T(8,128)S(1)} %copy.7.shape_ref, bf16[128,256]{1,0:T(8,128)(2,1)S(1)} %copy-done.2, bf16[128,256]{1,0:T(8,128)(2,1)S(1)} %copy-done.1, f32[2,32,128]{2,1,0:T(8,128)S(1)} %copy-done.3, bf16[32,192]{1,0:T(8,128)(2,1)S(1)} %copy-done.4), custom_call_target="tpu_custom_call" | custom-call | tf_op jit(solution)/shard_map/pallas_call | solution.py:305
  26.9 0.7 %copy.10 = f32[12,2,2048]{2,1,0:T(2,128)} copy(f32[12,2,2048]{2,1,0:T(2,128)S(1)} %bitcast.6) | data formatting | bytes 393216
Async XLA Ops:
  0.0 0.9 %copy-start.1 = (bf16[128,256]{1,0:T(8,128)(2,1)S(1)}, bf16[128,256]{1,0:T(8,128)(2,1)}, u32[]{:S(2)}) copy-start(bf16[128,256]{1,0:T(8,128)(2,1)} %constant.9.clone.first_lo) | copy-start | bytes 196612
  0.0 0.9 %copy-start.4 = (bf16[32,192]{1,0:T(8,128)(2,1)S(1)}, bf16[32,192]{1,0:T(8,128)(2,1)}, u32[]{:S(2)}) copy-start(bf16[32,192]{1,0:T(8,128)(2,1)} %constant.11.clone.second) | copy-start | bytes 36868
  0.9 1.0 %copy-start = (f32[512,128]{1,0:T(8,128)S(1)}, f32[512,128]{1,0:T(8,128)}, u32[]{:S(2)}) copy-start(f32[512,128]{1,0:T(8,128)} %param.6) | copy-start | bytes 786436
  1.8 0.8 %copy-start.2 = (bf16[128,256]{1,0:T(8,128)(2,1)S(1)}, bf16[128,256]{1,0:T(8,128)(2,1)}, u32[]{:S(2)}) copy-start(bf16[128,256]{1,0:T(8,128)(2,1)} %constant.8.clone.first_hi) | copy-start | bytes 196612
  2.7 0.8 %copy-start.3 = (f32[2,32,128]{2,1,0:T(8,128)S(1)}, f32[2,32,128]{2,1,0:T(8,128)}, u32[]{:S(2)}) copy-start(f32[2,32,128]{2,1,0:T(8,128)} %constant.10.clone.twist) | copy-start | bytes 98308

commit v2 on v1

--- a/solution.py
+++ b/solution.py
@@ -80,20 +80,20 @@
     two_pi = 2.0 * np.pi
     a = np.arange(RADIX)
     ang = two_pi * ((a[:, None] * a[None, :]) % RADIX) / RADIX
-    first = np.concatenate([np.cos(ang), -np.sin(ang)], axis=1)
-    first_hi, first_lo = split_np(first)
-    row = np.arange(REST)
-    b = (row % 4) * 8 + row // 4
-    twist = two_pi * ((b[:, None] * a[None, :]) % steps) / steps
+    parts = [np.cos(ang), -np.sin(ang)]
     k2 = np.arange(REST // 2)
-    last = two_pi * ((k2[:, None] * b[None, :]) % REST) / REST
-    real = np.concatenate([np.cos(last), np.sin(last)], axis=1)
-    imag = np.concatenate([-np.sin(last), np.cos(last)], axis=1)
-    second = np.stack([real, imag], axis=1).reshape(REST, 2 * REST) / math.sqrt(steps)
-    second_hi, second_lo = split_np(second)
-    second_all = np.concatenate([second_hi, second_hi, second_lo], axis=1)
-    twist_all = np.stack([np.cos(twist), np.sin(twist)]).astype(np.float32)
-    return first_hi, first_lo, twist_all, second_all
+    for c in range(2):
+        row = np.arange(REST // 2)
+        b = (2 * c + row % 2) * 8 + row // 2
+        twist = two_pi * ((b[:, None] * a[None, :]) % steps) / steps
+        parts += [np.cos(twist), np.sin(twist)]
+        last = two_pi * ((k2[:, None] * b[None, :]) % REST) / REST
+        real = np.concatenate([np.cos(last), np.sin(last)], axis=1)
+        imag = np.concatenate([-np.sin(last), np.cos(last)], axis=1)
+        second = np.stack([real, imag], axis=1).reshape(REST, REST) / math.sqrt(steps)
+        hi, lo = (p.astype(np.float64) for p in split_np(second))
+        parts.append(np.concatenate([hi, hi, lo, np.zeros_like(hi)], axis=1))
+    return np.concatenate(parts, axis=0).astype(np.float32)
 
 
 def split(x):
@@ -114,10 +114,12 @@
 
 def fused(
     elems, modes, width,
-    hist, shape_ref, first_hi, first_lo, twist, second,
+    hist, shapes, table,
     out,
-    hbuf, s_send, s_recv, gathered, s_all, outbox, inbox, turned,
-    own_sem, hs_sem, hr_sem, s1s_sem, s1r_sem, s2s_sem, s2r_sem, as_sem, ar_sem,
+    hbuf, h_his, h_los, own_shapes, s_send, s_recv, gathered, s_all, outbox, inbox,
+    turned, consts,
+    own_sem, fetch_sem, hs_sem, hr_sem, s1s_sem, s1r_sem, s2s_sem, s2r_sem,
+    as_sem, ar_sem,
 ):
     chunks = 2
     e = lax.axis_index("elem")
@@ -125,27 +127,32 @@
     sibling = m + 1 - 2 * (m % 2)
     across = (m + 2) % modes
     diagonal = (modes - 1) - m
+    beside = e + 1 - 2 * (e % 2)
+
+    fetch_shapes = pltpu.make_async_copy(shapes, own_shapes, fetch_sem.at[0])
+    fetch_table = pltpu.make_async_copy(table, consts, fetch_sem.at[1])
+    own = [
+        pltpu.make_async_copy(hist.at[:, c], hbuf.at[m, c], own_sem.at[c])
+        for c in range(chunks)
+    ]
+    fetch_shapes.start()
+    for copy in own:
+        copy.start()
+    fetch_table.start()
 
     barrier = pltpu.get_barrier_semaphore()
-    for peer in (sibling, across, diagonal):
-        pl.semaphore_signal(barrier, inc=1, device_id=(e, peer), device_id_type=MESH)
     for d in range(1, elems):
         pl.semaphore_signal(
             barrier, inc=1, device_id=((e + d) % elems, m), device_id_type=MESH
         )
-
-    own = [
-        pltpu.make_async_copy(hist.at[:, c], hbuf.at[m, c], own_sem.at[c])
-        for c in range(chunks)
-    ]
-    for copy in own:
-        copy.start()
-
-    modes_t = shape_ref[...].T
+    for peer in (across, diagonal, sibling):
+        pl.semaphore_signal(barrier, inc=1, device_id=(e, peer), device_id_type=MESH)
+
+    s_all[...] = jnp.zeros_like(s_all)
+    fetch_shapes.wait()
     for p in range(modes):
-        s_send[p, :width, :] = modes_t[p * width : (p + 1) * width, :]
+        s_send[p, :width, :] = own_shapes[p * width : (p + 1) * width, :]
     s_recv[m, :width, :] = s_send[m, :width, :]
-    s_all[...] = jnp.zeros_like(s_all)
 
     pl.semaphore_wait(barrier, modes - 1 + elems - 1)
 
@@ -181,32 +188,55 @@
         to_across[c].start()
         to_sibling[c].start()
 
+    def split_history(origin, c):
+        flat = hbuf.at[origin, c].reshape(256, 128)
+        turned_rows = [flat[pl.ds(i, 16, stride=16), :] for i in range(16)]
+        hi, lo = split(jnp.concatenate(turned_rows, axis=0))
+        h_his[c, origin] = hi
+        h_los[c, origin] = lo
+
+    own[0].wait()
+    split_history(m, 0)
+
     for _, landed in first_copies:
         landed.wait_recv()
     for p in range(modes):
         gathered[e, p * width : (p + 1) * width, :] = s_recv[p, :width, :]
 
-    order = sorted(range(1, elems), key=lambda d: -min(d, elems - d))
-    second_copies = []
-    for d in order:
-        peer, source = (e + d) % elems, (e + elems - d) % elems
-        copy = pltpu.make_async_remote_copy(
-            gathered.at[e], gathered.at[e], s2s_sem.at[d], s2r_sem.at[d],
+    def shape_copy(slot, block, peer):
+        return pltpu.make_async_remote_copy(
+            gathered.at[block], gathered.at[block], s2s_sem.at[slot], s2r_sem.at[slot],
             device_id=(peer, m), device_id_type=MESH,
         )
-        landed = pltpu.make_async_remote_copy(
-            gathered.at[source], gathered.at[source], s2s_sem.at[d], s2r_sem.at[d],
-            device_id=(peer, m), device_id_type=MESH,
-        )
+
+    shape_sends = []
+    steps_z = [elems // 2] + [d for d in range(2, elems, 2) if d != elems // 2]
+    for d in steps_z:
+        shape_sends.append(shape_copy(d, e, (e + d) % elems))
+    shape_sends.append(shape_copy(1, e, beside))
+    for copy in shape_sends:
         copy.start()
-        second_copies.append((copy, landed))
-
+
+    own[1].wait()
+    split_history(m, 1)
     for c in range(chunks):
-        from_across[c].wait_recv()
-        forward[c].start()
-
-    for _, landed in second_copies:
-        landed.wait_recv()
+        from_sibling[c].wait_recv()
+        split_history(sibling, c)
+
+    for d in sorted(steps_z, key=lambda d: min(d, elems - d)):
+        source = (e + elems - d) % elems
+        shape_copy(d, source, source).wait_recv()
+        copy = shape_copy(d + 1, source, beside)
+        copy.start()
+        shape_sends.append(copy)
+
+    from_across[0].wait_recv()
+    forward[0].start()
+    split_history(across, 0)
+
+    shape_copy(1, beside, beside).wait_recv()
+    for d in steps_z:
+        shape_copy(d + 1, (beside + elems - d) % elems, beside).wait_recv()
     for owner in range(elems):
         for p in range(modes):
             s_all[owner * 16 : owner * 16 + width, p * 128 : (p + 1) * 128] = (
@@ -216,20 +246,17 @@
     s_both = jnp.concatenate([s_hi, s_lo], axis=0)
     rows = s_hi.shape[0]
 
+    order = sorted(range(1, elems), key=lambda d: -min(d, elems - d))
     last_copies = []
     for c in range(chunks):
-        own[c].wait()
-        from_sibling[c].wait_recv()
+        if c:
+            from_across[c].wait_recv()
+            forward[c].start()
+            split_history(across, c)
         from_forward[c].wait_recv()
-        pieces = []
-        for p in range(modes):
-            flat = hbuf.at[p, c].reshape(256, 128)
-            pieces.append(
-                jnp.concatenate(
-                    [flat[pl.ds(i, 16, stride=16), :] for i in range(16)], axis=0
-                )
-            )
-        h_hi, h_lo = split(jnp.concatenate(pieces, axis=1))
+        split_history(diagonal, c)
+        h_hi = jnp.concatenate([h_his[c, p] for p in range(modes)], axis=1)
+        h_lo = jnp.concatenate([h_los[c, p] for p in range(modes)], axis=1)
         both = nt(s_both, h_hi)
         stress = both[:rows] + (both[rows:] + nt(s_hi, h_lo))
         for owner in range(elems):
@@ -248,49 +275,61 @@
                 ar_sem.at[d, c], device_id=(peer, m), device_id_type=MESH,
             )
             copy.start()
-            last_copies.append((copy, landed))
+            last_copies.append((c, copy, landed))
         inbox[e, c] = outbox[e, c]
 
-    for _, landed in last_copies:
-        landed.wait_recv()
-
-    blocks = [
-        jnp.concatenate([inbox[i, 0], inbox[i, 1]], axis=0) for i in range(elems)
-    ]
-    group = lax.broadcasted_iota(jnp.int32, blocks[0].shape, 1) // 16
-    for step in (4, 2, 1):
-        low = (group // step) % 2 == 0
-        for i in range(elems):
-            if (i // step) % 2 == 0:
-                one, two = blocks[i], blocks[i + step]
-                blocks[i] = jnp.where(low, one, pltpu.roll(two, 16 * step, 1))
-                blocks[i + step] = jnp.where(
-                    low, pltpu.roll(one, 128 - 16 * step, 1), two
-                )
-    x_hi, x_lo = split(jnp.concatenate(blocks, axis=0))
-    w_hi, w_lo = first_hi[...], first_lo[...]
-    once = nn(x_hi, w_hi) + (nn(x_lo, w_hi) + nn(x_hi, w_lo))
-    turned[0] = once[:, :128]
-    turned[1] = once[:, 128:]
-
-    cos, sin = twist[0], twist[1]
-    real, imag = [], []
-    for col in range(width):
-        re = turned.at[0][pl.ds(col, REST, stride=width), :]
-        im = turned.at[1][pl.ds(col, REST, stride=width), :]
-        real.append(re * cos + im * sin)
-        imag.append(im * cos - re * sin)
-    z = jnp.concatenate(
-        [jnp.concatenate(real, axis=1), jnp.concatenate(imag, axis=1)], axis=0
-    )
-    z_hi, z_lo = split(z)
-    result = nn(second[...], jnp.concatenate([z_hi, z_lo, z_hi], axis=0))
-    for col in range(width):
-        out[col] = result[:, col * 128 : (col + 1) * 128]
-
-    for copy, _ in first_copies + second_copies + last_copies:
+    fetch_table.wait()
+    w_hi, w_lo = split(
+        jnp.concatenate([consts[:128, :], consts[128:256, :]], axis=1)
+    )
+    half = REST // 2
+    total = None
+    for c in range(chunks):
+        for chunk, _, landed in last_copies:
+            if chunk == c:
+                landed.wait_recv()
+        blocks = [inbox[i, c] for i in range(elems)]
+        group = lax.broadcasted_iota(jnp.int32, blocks[0].shape, 1) // 16
+        for step in (4, 2, 1):
+            low = (group // step) % 2 == 0
+            for i in range(elems):
+                if (i // step) % 2 == 0:
+                    one, two = blocks[i], blocks[i + step]
+                    blocks[i] = jnp.where(low, one, pltpu.roll(two, 16 * step, 1))
+                    blocks[i + step] = jnp.where(
+                        low, pltpu.roll(one, 128 - 16 * step, 1), two
+                    )
+        x_hi, x_lo = split(jnp.concatenate(blocks, axis=0))
+        once = nn(x_hi, w_hi) + (nn(x_lo, w_hi) + nn(x_hi, w_lo))
+        turned[c, 0] = once[:, :128]
+        turned[c, 1] = once[:, 128:]
+        base = 256 + c * (REST + REST)
+        cos = consts[base : base + half, :]
+        sin = consts[base + half : base + REST, :]
+        second = consts[base + REST : base + 2 * REST, : 3 * REST].astype(bf16)
+        real, imag = [], []
+        for col in range(width):
+            re = turned.at[c, 0][pl.ds(col, half, stride=width), :]
+            im = turned.at[c, 1][pl.ds(col, half, stride=width), :]
+            real.append(re * cos + im * sin)
+            imag.append(im * cos - re * sin)
+        z = jnp.concatenate(
+            [jnp.concatenate(real, axis=1), jnp.concatenate(imag, axis=1)], axis=0
+        )
+        z_hi, z_lo = split(z)
+        part = nn(second, jnp.concatenate([z_hi, z_lo, z_hi], axis=0))
+        if c == 0:
+            for col in range(width):
+                out[col] = part[:, col * 128 : (col + 1) * 128]
+        else:
+            for col in range(width):
+                out[col] += part[:, col * 128 : (col + 1) * 128]
+
+    for copy, _ in first_copies:
         copy.wait_send()
-    for copy in to_across + to_sibling + forward:
+    for _, copy, _ in last_copies:
+        copy.wait_send()
+    for copy in shape_sends + to_across + to_sibling + forward:
         copy.wait_send()
 
 
@@ -298,34 +337,38 @@
     elems, modes = lax.axis_size("elem"), lax.axis_size("mode")
     steps = modal_history.shape[0] * elems
     width = stress_modes.shape[1] // modes
-    consts = [jnp.asarray(t) for t in tables(steps)]
+    table = jnp.asarray(tables(steps))
     hist = modal_history.reshape(16, 2, 16, 128)
-    vmem = pl.BlockSpec(memory_space=pltpu.VMEM)
+    hbm = pl.BlockSpec(memory_space=pl.ANY)
     dma = pltpu.SemaphoreType.DMA
     result = pl.pallas_call(
         functools.partial(fused, elems, modes, width),
         out_shape=jax.ShapeDtypeStruct((width, REST, RADIX), f32),
-        in_specs=[pl.BlockSpec(memory_space=pl.ANY)] + [vmem] * 5,
-        out_specs=vmem,
+        in_specs=[hbm] * 3,
+        out_specs=pl.BlockSpec(memory_space=pltpu.VMEM),
         scratch_shapes=[
             pltpu.VMEM((modes, 2, 16, 16, 128), f32),
+            pltpu.VMEM((2, modes, 256, 128), bf16),
+            pltpu.VMEM((2, modes, 256, 128), bf16),
+            pltpu.VMEM((modes * width, 128), f32),
             pltpu.VMEM((modes, 16, 128), f32),
             pltpu.VMEM((modes, 16, 128), f32),
             pltpu.VMEM((elems, modes * width, 128), f32),
             pltpu.VMEM((elems * 16, modes * 128), f32),
             pltpu.VMEM((elems, 2, 2 * width, 128), f32),
             pltpu.VMEM((elems, 2, 2 * width, 128), f32),
-            pltpu.VMEM((2, REST * width, 128), f32),
-            dma((2,)),
+            pltpu.VMEM((2, 2, REST // 2 * width, 128), f32),
+            pltpu.VMEM(table.shape, f32),
+            dma((2,)), dma((2,)),
             dma((3, 2)), dma((3, 2)),
             dma((3,)), dma((3,)),
             dma((elems,)), dma((elems,)),
             dma((elems, 2)), dma((elems, 2)),
         ],
         compiler_params=pltpu.CompilerParams(
-            collective_id=0, has_side_effects=True, vmem_limit_bytes=32 * 1024 * 1024
+            collective_id=0, has_side_effects=True, vmem_limit_bytes=60 * 1024 * 1024
         ),
-    )(hist, stress_modes, *consts)
+    )(hist, stress_modes.T, table)
     ordered = result.reshape(width, REST // 2, 2, RADIX).transpose(0, 2, 1, 3)
     return ordered.reshape(width, 2, REST // 2 * RADIX)
 

time: 27.9 us -> 27.1 us (0.971)
  local copies, waits for them, and re-layouts: 4.09 us -> 1.62 us
  Pallas kernels: 23.4 us -> 25.3 us
    unnamed x12 -> x1, local copies, waits for them, and re-layouts: 4.09 us -> 1.62 us
    pallas_call x1, Pallas kernels: 23.4 us -> 25.3 us  [with_kernel(): pl.pallas_call(functools.partial(fused, elems, modes, width), out_shape=j...]
where the time goes in v2:
time: 27.1 us; the launch traced here: 26.9 us
  Pallas kernels  25.3 us (93%)
  local copies, waits for them, and re-layouts  1.62 us (6%)
    pallas_call x1, Pallas kernels, with_kernel(): pl.pallas_call(functools.partial(fused, elems, modes, width), out_shape=j...  25.3 us
    unnamed x1, local copies, waits for them, and re-layouts  1.62 us

profile of v2, /device:TPU:0, one launch (start us, length us, event | category | flops | bytes accessed | tf_op | source)
XLA Modules:
  0.0 26.9 jit_solution(12078701402956931242)
XLA Ops:
  0.0 25.3 %shard_map.37 = f32[12,32,128]{2,1,0:T(8,128)} custom-call(f32[16,2,16,128]{3,2,1,0:T(8,128)} %bitcast.8, f32[48,128]{1,0:T(8,128)} %bitcast.9, f32[384,128]{1,0:T(8,128)} %constant.2.clone.table), custom_call_target="tpu_custom_call" | custom-call | tf_op jit(solution)/shard_map/pallas_call | solution.py:344
  25.3 1.6 %copy.6 = f32[12,2,2048]{2,1,0:T(2,128)} copy(f32[12,2,2048]{2,1,0:T(2,128)} %bitcast.7) | data formatting | bytes 393216

commit v3 on v2

--- a/solution.py
+++ b/solution.py
@@ -116,23 +116,26 @@
     elems, modes, width,
     hist, shapes, table,
     out,
-    hbuf, h_his, h_los, own_shapes, s_send, s_recv, gathered, s_all, outbox, inbox,
+    hbuf, h_his, h_los, gathered, parts, other_parts, outbox, inbox,
     turned, consts,
     own_sem, fetch_sem, hs_sem, hr_sem, s1s_sem, s1r_sem, s2s_sem, s2r_sem,
-    as_sem, ar_sem,
+    ps_sem, pr_sem, as_sem, ar_sem,
 ):
     chunks = 2
     e = lax.axis_index("elem")
     m = lax.axis_index("mode")
-    sibling = m + 1 - 2 * (m % 2)
+    x, core = m // 2, m % 2
+    sibling = m + 1 - 2 * core
     across = (m + 2) % modes
-    diagonal = (modes - 1) - m
     beside = e + 1 - 2 * (e % 2)
-
-    fetch_shapes = pltpu.make_async_copy(shapes, own_shapes, fetch_sem.at[0])
+    halves = (x, 1 - x)
+
+    fetch_shapes = pltpu.make_async_copy(
+        shapes.at[x], gathered.at[e, x], fetch_sem.at[0]
+    )
     fetch_table = pltpu.make_async_copy(table, consts, fetch_sem.at[1])
     own = [
-        pltpu.make_async_copy(hist.at[:, c], hbuf.at[m, c], own_sem.at[c])
+        pltpu.make_async_copy(hist.at[:, c], hbuf.at[x, c], own_sem.at[c])
         for c in range(chunks)
     ]
     fetch_shapes.start()
@@ -145,48 +148,52 @@
         pl.semaphore_signal(
             barrier, inc=1, device_id=((e + d) % elems, m), device_id_type=MESH
         )
-    for peer in (across, diagonal, sibling):
+    for peer in (across, sibling):
         pl.semaphore_signal(barrier, inc=1, device_id=(e, peer), device_id_type=MESH)
-
-    s_all[...] = jnp.zeros_like(s_all)
+    pl.semaphore_wait(barrier, elems - 1 + 2)
+
+    to_regroup = pltpu.make_async_remote_copy(
+        shapes.at[1 - x], gathered.at[e, x], s1s_sem.at[0], s1r_sem.at[0],
+        device_id=(e, across), device_id_type=MESH,
+    )
+    from_regroup = pltpu.make_async_remote_copy(
+        shapes.at[1 - x], gathered.at[e, 1 - x], s1s_sem.at[0], s1r_sem.at[0],
+        device_id=(e, across), device_id_type=MESH,
+    )
+    to_regroup.start()
+
+    def shape_copy(slot, block, kind, peer):
+        ref = gathered.at[block, halves[kind]]
+        return pltpu.make_async_remote_copy(
+            ref, ref, s2s_sem.at[slot, kind], s2r_sem.at[slot, kind],
+            device_id=(peer, m), device_id_type=MESH,
+        )
+
+    shape_sends = []
+    steps_z = [elems // 2] + [d for d in range(2, elems, 2) if d != elems // 2]
+
+    def send_shapes(kind):
+        for d in steps_z:
+            shape_sends.append(shape_copy(d, e, kind, (e + d) % elems))
+            shape_sends[-1].start()
+        shape_sends.append(shape_copy(1, e, kind, beside))
+        shape_sends[-1].start()
+
     fetch_shapes.wait()
-    for p in range(modes):
-        s_send[p, :width, :] = own_shapes[p * width : (p + 1) * width, :]
-    s_recv[m, :width, :] = s_send[m, :width, :]
-
-    pl.semaphore_wait(barrier, modes - 1 + elems - 1)
-
-    first_copies = []
-    for i, peer in enumerate((across, diagonal, sibling)):
-        first_copies.append((
+    send_shapes(0)
+
+    to_across, from_across = [
+        [
             pltpu.make_async_remote_copy(
-                s_send.at[peer], s_recv.at[m], s1s_sem.at[i], s1r_sem.at[i],
-                device_id=(e, peer), device_id_type=MESH,
-            ),
-            pltpu.make_async_remote_copy(
-                s_send.at[peer], s_recv.at[peer], s1s_sem.at[i], s1r_sem.at[i],
-                device_id=(e, peer), device_id_type=MESH,
-            ),
-        ))
-    for copy, _ in first_copies:
+                hist.at[:, c], hbuf.at[origin, c], hs_sem.at[c], hr_sem.at[c],
+                device_id=(e, across), device_id_type=MESH,
+            )
+            for c in range(chunks)
+        ]
+        for origin in (x, 1 - x)
+    ]
+    for copy in to_across:
         copy.start()
-
-    def history_copy(kind, c, origin, peer):
-        src = hist.at[:, c] if kind < 2 else hbuf.at[origin, c]
-        return pltpu.make_async_remote_copy(
-            src, hbuf.at[origin, c], hs_sem.at[kind, c], hr_sem.at[kind, c],
-            device_id=(e, peer), device_id_type=MESH,
-        )
-
-    to_across = [history_copy(0, c, m, across) for c in range(chunks)]
-    to_sibling = [history_copy(1, c, m, sibling) for c in range(chunks)]
-    forward = [history_copy(2, c, across, sibling) for c in range(chunks)]
-    from_across = [history_copy(0, c, across, across) for c in range(chunks)]
-    from_sibling = [history_copy(1, c, sibling, sibling) for c in range(chunks)]
-    from_forward = [history_copy(2, c, diagonal, sibling) for c in range(chunks)]
-    for c in range(chunks):
-        to_across[c].start()
-        to_sibling[c].start()
 
     def split_history(origin, c):
         flat = hbuf.at[origin, c].reshape(256, 128)
@@ -195,88 +202,79 @@
         h_his[c, origin] = hi
         h_los[c, origin] = lo
 
-    own[0].wait()
-    split_history(m, 0)
-
-    for _, landed in first_copies:
-        landed.wait_recv()
-    for p in range(modes):
-        gathered[e, p * width : (p + 1) * width, :] = s_recv[p, :width, :]
-
-    def shape_copy(slot, block, peer):
-        return pltpu.make_async_remote_copy(
-            gathered.at[block], gathered.at[block], s2s_sem.at[slot], s2r_sem.at[slot],
-            device_id=(peer, m), device_id_type=MESH,
-        )
-
-    shape_sends = []
-    steps_z = [elems // 2] + [d for d in range(2, elems, 2) if d != elems // 2]
-    for d in steps_z:
-        shape_sends.append(shape_copy(d, e, (e + d) % elems))
-    shape_sends.append(shape_copy(1, e, beside))
-    for copy in shape_sends:
-        copy.start()
-
-    own[1].wait()
-    split_history(m, 1)
+    from_regroup.wait_recv()
+    send_shapes(1)
     for c in range(chunks):
-        from_sibling[c].wait_recv()
-        split_history(sibling, c)
-
-    for d in sorted(steps_z, key=lambda d: min(d, elems - d)):
-        source = (e + elems - d) % elems
-        shape_copy(d, source, source).wait_recv()
-        copy = shape_copy(d + 1, source, beside)
-        copy.start()
-        shape_sends.append(copy)
+        own[c].wait()
+        split_history(x, c)
+
+    for kind in range(2):
+        for d in sorted(steps_z, key=lambda d: min(d, elems - d)):
+            source = (e + elems - d) % elems
+            shape_copy(d, source, kind, source).wait_recv()
+            copy = shape_copy(d + 1, source, kind, beside)
+            copy.start()
+            shape_sends.append(copy)
 
     from_across[0].wait_recv()
-    forward[0].start()
-    split_history(across, 0)
-
-    shape_copy(1, beside, beside).wait_recv()
-    for d in steps_z:
-        shape_copy(d + 1, (beside + elems - d) % elems, beside).wait_recv()
-    for owner in range(elems):
-        for p in range(modes):
-            s_all[owner * 16 : owner * 16 + width, p * 128 : (p + 1) * 128] = (
-                gathered[owner, p * width : (p + 1) * width, :]
-            )
-    s_hi, s_lo = split(s_all[...])
+    split_history(1 - x, 0)
+
+    for kind in range(2):
+        shape_copy(1, beside, kind, beside).wait_recv()
+        for d in steps_z:
+            source = (beside + elems - d) % elems
+            shape_copy(d + 1, source, kind, beside).wait_recv()
+    s_hi, s_lo = split(
+        jnp.concatenate(
+            [
+                jnp.concatenate([gathered[owner, h] for h in range(2)], axis=1)
+                for owner in range(elems)
+            ],
+            axis=0,
+        )
+    )
     s_both = jnp.concatenate([s_hi, s_lo], axis=0)
     rows = s_hi.shape[0]
 
     order = sorted(range(1, elems), key=lambda d: -min(d, elems - d))
-    last_copies = []
+    last_copies, part_copies = [], []
     for c in range(chunks):
         if c:
             from_across[c].wait_recv()
-            forward[c].start()
-            split_history(across, c)
-        from_forward[c].wait_recv()
-        split_history(diagonal, c)
-        h_hi = jnp.concatenate([h_his[c, p] for p in range(modes)], axis=1)
-        h_lo = jnp.concatenate([h_los[c, p] for p in range(modes)], axis=1)
+            split_history(1 - x, c)
+        h_hi = jnp.concatenate([h_his[c, h] for h in range(2)], axis=1)
+        h_lo = jnp.concatenate([h_los[c, h] for h in range(2)], axis=1)
         both = nt(s_both, h_hi)
         stress = both[:rows] + (both[rows:] + nt(s_hi, h_lo))
         for owner in range(elems):
-            for h in range(2):
-                outbox[owner, c, h * width : (h + 1) * width, :] = stress[
-                    owner * 16 : owner * 16 + width, h * 128 : (h + 1) * 128
-                ]
+            for k in range(2):
+                for h in range(2):
+                    start = (owner * 2 + k) * width
+                    parts[c, k, owner, h * width : (h + 1) * width, :] = stress[
+                        start : start + width, h * 128 : (h + 1) * 128
+                    ]
+        copy = pltpu.make_async_remote_copy(
+            parts.at[c, 1 - core], other_parts.at[c], ps_sem.at[c], pr_sem.at[c],
+            device_id=(e, sibling), device_id_type=MESH,
+        )
+        copy.start()
+        part_copies.append(copy)
+        copy.wait_recv()
+        whole = parts[c, core] + other_parts[c]
+        outbox[c] = whole
         for d in order:
             peer, source = (e + d) % elems, (e + elems - d) % elems
             copy = pltpu.make_async_remote_copy(
-                outbox.at[peer, c], inbox.at[e, c], as_sem.at[d, c], ar_sem.at[d, c],
+                outbox.at[c, peer], inbox.at[c, e], as_sem.at[d, c], ar_sem.at[d, c],
                 device_id=(peer, m), device_id_type=MESH,
             )
             landed = pltpu.make_async_remote_copy(
-                outbox.at[peer, c], inbox.at[source, c], as_sem.at[d, c],
+                outbox.at[c, peer], inbox.at[c, source], as_sem.at[d, c],
                 ar_sem.at[d, c], device_id=(peer, m), device_id_type=MESH,
             )
             copy.start()
             last_copies.append((c, copy, landed))
-        inbox[e, c] = outbox[e, c]
+        inbox[c, e] = outbox[c, e]
 
     fetch_table.wait()
     w_hi, w_lo = split(
@@ -288,7 +286,7 @@
         for chunk, _, landed in last_copies:
             if chunk == c:
                 landed.wait_recv()
-        blocks = [inbox[i, c] for i in range(elems)]
+        blocks = [inbox[c, i] for i in range(elems)]
         group = lax.broadcasted_iota(jnp.int32, blocks[0].shape, 1) // 16
         for step in (4, 2, 1):
             low = (group // step) % 2 == 0
@@ -325,11 +323,9 @@
             for col in range(width):
                 out[col] += part[:, col * 128 : (col + 1) * 128]
 
-    for copy, _ in first_copies:
-        copy.wait_send()
     for _, copy, _ in last_copies:
         copy.wait_send()
-    for copy in shape_sends + to_across + to_sibling + forward:
+    for copy in [to_regroup] + shape_sends + to_across + part_copies:
         copy.wait_send()
 
 
@@ -339,6 +335,7 @@
     width = stress_modes.shape[1] // modes
     table = jnp.asarray(tables(steps))
     hist = modal_history.reshape(16, 2, 16, 128)
+    shapes = stress_modes.T.reshape(2, 2 * width, 128)
     hbm = pl.BlockSpec(memory_space=pl.ANY)
     dma = pltpu.SemaphoreType.DMA
     result = pl.pallas_call(
@@ -347,28 +344,27 @@
         in_specs=[hbm] * 3,
         out_specs=pl.BlockSpec(memory_space=pltpu.VMEM),
         scratch_shapes=[
-            pltpu.VMEM((modes, 2, 16, 16, 128), f32),
-            pltpu.VMEM((2, modes, 256, 128), bf16),
-            pltpu.VMEM((2, modes, 256, 128), bf16),
-            pltpu.VMEM((modes * width, 128), f32),
-            pltpu.VMEM((modes, 16, 128), f32),
-            pltpu.VMEM((modes, 16, 128), f32),
-            pltpu.VMEM((elems, modes * width, 128), f32),
-            pltpu.VMEM((elems * 16, modes * 128), f32),
+            pltpu.VMEM((2, 2, 16, 16, 128), f32),
+            pltpu.VMEM((2, 2, 256, 128), bf16),
+            pltpu.VMEM((2, 2, 256, 128), bf16),
             pltpu.VMEM((elems, 2, 2 * width, 128), f32),
-            pltpu.VMEM((elems, 2, 2 * width, 128), f32),
+            pltpu.VMEM((2, 2, elems, 2 * width, 128), f32),
+            pltpu.VMEM((2, elems, 2 * width, 128), f32),
+            pltpu.VMEM((2, elems, 2 * width, 128), f32),
+            pltpu.VMEM((2, elems, 2 * width, 128), f32),
             pltpu.VMEM((2, 2, REST // 2 * width, 128), f32),
             pltpu.VMEM(table.shape, f32),
             dma((2,)), dma((2,)),
-            dma((3, 2)), dma((3, 2)),
-            dma((3,)), dma((3,)),
-            dma((elems,)), dma((elems,)),
+            dma((2,)), dma((2,)),
+            dma((1,)), dma((1,)),
+            dma((elems, 2)), dma((elems, 2)),
+            dma((2,)), dma((2,)),
             dma((elems, 2)), dma((elems, 2)),
         ],
         compiler_params=pltpu.CompilerParams(
-            collective_id=0, has_side_effects=True, vmem_limit_bytes=60 * 1024 * 1024
+            collective_id=0, has_side_effects=True, vmem_limit_bytes=55000 * 1024
         ),
-    )(hist, stress_modes.T, table)
+    )(hist, shapes, table)
     ordered = result.reshape(width, REST // 2, 2, RADIX).transpose(0, 2, 1, 3)
     return ordered.reshape(width, 2, REST // 2 * RADIX)
 

time: 27.1 us -> 26.5 us (0.978)
  Pallas kernels: 25.3 us -> 24.9 us
    pallas_call x1, Pallas kernels: 25.3 us -> 24.9 us  [with_kernel(): pl.pallas_call(functools.partial(fused, elems, modes, width), out_shape=j...]
    unnamed x1 -> x3, local copies, waits for them, and re-layouts: 1.62 us -> 1.42 us
where the time goes in v3:
time: 26.5 us; the launch traced here: 26.3 us
  Pallas kernels  24.9 us (94%)
  local copies, waits for them, and re-layouts  1.42 us (5%)
    pallas_call x1, Pallas kernels, with_kernel(): pl.pallas_call(functools.partial(fused, elems, modes, width), out_shape=j...  24.9 us
    unnamed x3, local copies, waits for them, and re-layouts  1.42 us

profile of v3, /device:TPU:0, one launch (start us, length us, event | category | flops | bytes accessed | tf_op | source)
XLA Modules:
  0.0 26.3 jit_solution(1869777090266992742)
XLA Ops:
  0.0 0.0 copy-start
  0.0 0.7 %copy-done = f32[128,48]{0,1:T(8,128)S(1)} copy-done((f32[128,48]{0,1:T(8,128)S(1)}, f32[128,48]{0,1:T(8,128)}, u32[]{:S(2)}) %copy-start) | copy-done | bytes 24600
  0.7 24.9 %shard_map.37 = f32[12,32,128]{2,1,0:T(8,128)S(1)} custom-call(f32[16,2,16,128]{3,2,1,0:T(8,128)} %bitcast.11, f32[2,24,128]{2,1,0:T(8,128)S(1)} %bitcast.10, f32[384,128]{1,0:T(8,128)} %constant.2.clone.table), custom_call_target="tpu_custom_call" | custom-call | tf_op jit(solution)/shard_map/pallas_call | solution.py:341
  25.6 0.7 %copy.6 = f32[12,2,2048]{2,1,0:T(2,128)} copy(f32[12,2,2048]{2,1,0:T(2,128)S(1)} %bitcast.9) | data formatting | bytes 393216
Async XLA Ops:
  0.0 0.7 %copy-start = (f32[128,48]{0,1:T(8,128)S(1)}, f32[128,48]{0,1:T(8,128)}, u32[]{:S(2)}) copy-start(f32[128,48]{0,1:T(8,128)} %param.4) | copy-start | bytes 73732

commit v4 on v3

--- a/solution.py
+++ b/solution.py
@@ -118,7 +118,7 @@
     out,
     hbuf, h_his, h_los, gathered, parts, other_parts, outbox, inbox,
     turned, consts,
-    own_sem, fetch_sem, hs_sem, hr_sem, s1s_sem, s1r_sem, s2s_sem, s2r_sem,
+    own_sem, fetch_sem, hs_sem, hr_sem, s1s_sem, s1r_sem, z_send, z_recv, y_send, y_recv,
     ps_sem, pr_sem, as_sem, ar_sem,
 ):
     chunks = 2
@@ -129,6 +129,7 @@
     across = (m + 2) % modes
     beside = e + 1 - 2 * (e % 2)
     halves = (x, 1 - x)
+    z, top = e // 2, elems // 2 - 1
 
     fetch_shapes = pltpu.make_async_copy(
         shapes.at[x], gathered.at[e, x], fetch_sem.at[0]
@@ -143,14 +144,26 @@
         copy.start()
     fetch_table.start()
 
+    below, above = z > 0, z < top
     barrier = pltpu.get_barrier_semaphore()
-    for d in range(1, elems):
-        pl.semaphore_signal(
-            barrier, inc=1, device_id=((e + d) % elems, m), device_id_type=MESH
-        )
-    for peer in (across, sibling):
-        pl.semaphore_signal(barrier, inc=1, device_id=(e, peer), device_id_type=MESH)
-    pl.semaphore_wait(barrier, elems - 1 + 2)
+
+    def greet(device):
+        pl.semaphore_signal(barrier, inc=1, device_id=device, device_id_type=MESH)
+
+    greet((e, across))
+    greet((e, sibling))
+    greet((beside, m))
+
+    @pl.when(below)
+    def _():
+        greet((e - 2, m))
+
+    @pl.when(above)
+    def _():
+        greet((e + 2, m))
+
+    at_end = (z == 0).astype(jnp.int32) + (z == top).astype(jnp.int32)
+    pl.semaphore_wait(barrier, 5 - at_end)
 
     to_regroup = pltpu.make_async_remote_copy(
         shapes.at[1 - x], gathered.at[e, x], s1s_sem.at[0], s1r_sem.at[0],
@@ -162,22 +175,51 @@
     )
     to_regroup.start()
 
-    def shape_copy(slot, block, kind, peer):
+    def along(way, distance, kind, block, peer):
         ref = gathered.at[block, halves[kind]]
         return pltpu.make_async_remote_copy(
-            ref, ref, s2s_sem.at[slot, kind], s2r_sem.at[slot, kind],
+            ref, ref, z_send.at[way, distance, kind], z_recv.at[way, distance, kind],
             device_id=(peer, m), device_id_type=MESH,
         )
 
-    shape_sends = []
-    steps_z = [elems // 2] + [d for d in range(2, elems, 2) if d != elems // 2]
+    def aside(level, kind, block):
+        ref = gathered.at[block, halves[kind]]
+        return pltpu.make_async_remote_copy(
+            ref, ref, y_send.at[level, kind], y_recv.at[level, kind],
+            device_id=(beside, m), device_id_type=MESH,
+        )
+
+    def pass_on(way, distance, kind, act):
+        if way == 0:
+            @pl.when(above & (z >= distance))
+            def _():
+                act(along(0, distance, kind, e - 2 * distance, e + 2))
+        else:
+            @pl.when(below & (z + distance <= top))
+            def _():
+                act(along(1, distance, kind, e + 2 * distance, e - 2))
 
     def send_shapes(kind):
-        for d in steps_z:
-            shape_sends.append(shape_copy(d, e, kind, (e + d) % elems))
-            shape_sends[-1].start()
-        shape_sends.append(shape_copy(1, e, kind, beside))
-        shape_sends[-1].start()
+        for way in range(2):
+            pass_on(way, 0, kind, lambda copy: copy.start())
+        aside(z, kind, e).start()
+
+    def relay(distance, kind):
+        @pl.when(z >= distance)
+        def _():
+            block = e - 2 * distance
+            along(0, distance - 1, kind, block, e - 2).wait_recv()
+            if distance < top:
+                pass_on(0, distance, kind, lambda copy: copy.start())
+            aside(z - distance, kind, block).start()
+
+        @pl.when(z + distance <= top)
+        def _():
+            block = e + 2 * distance
+            along(1, distance - 1, kind, block, e + 2).wait_recv()
+            if distance < top:
+                pass_on(1, distance, kind, lambda copy: copy.start())
+            aside(z + distance, kind, block).start()
 
     fetch_shapes.wait()
     send_shapes(0)
@@ -208,22 +250,16 @@
         own[c].wait()
         split_history(x, c)
 
-    for kind in range(2):
-        for d in sorted(steps_z, key=lambda d: min(d, elems - d)):
-            source = (e + elems - d) % elems
-            shape_copy(d, source, kind, source).wait_recv()
-            copy = shape_copy(d + 1, source, kind, beside)
-            copy.start()
-            shape_sends.append(copy)
+    for distance in range(1, top + 1):
+        for kind in range(2):
+            relay(distance, kind)
 
     from_across[0].wait_recv()
     split_history(1 - x, 0)
 
     for kind in range(2):
-        shape_copy(1, beside, kind, beside).wait_recv()
-        for d in steps_z:
-            source = (beside + elems - d) % elems
-            shape_copy(d + 1, source, kind, beside).wait_recv()
+        for level in range(top + 1):
+            aside(level, kind, 2 * level + beside % 2).wait_recv()
     s_hi, s_lo = split(
         jnp.concatenate(
             [
@@ -311,10 +347,10 @@
             im = turned.at[c, 1][pl.ds(col, half, stride=width), :]
             real.append(re * cos + im * sin)
             imag.append(im * cos - re * sin)
-        z = jnp.concatenate(
+        waves = jnp.concatenate(
             [jnp.concatenate(real, axis=1), jnp.concatenate(imag, axis=1)], axis=0
         )
-        z_hi, z_lo = split(z)
+        z_hi, z_lo = split(waves)
         part = nn(second, jnp.concatenate([z_hi, z_lo, z_hi], axis=0))
         if c == 0:
             for col in range(width):
@@ -325,8 +361,14 @@
 
     for _, copy, _ in last_copies:
         copy.wait_send()
-    for copy in [to_regroup] + shape_sends + to_across + part_copies:
+    for copy in [to_regroup] + to_across + part_copies:
         copy.wait_send()
+    for kind in range(2):
+        for distance in range(top):
+            for way in range(2):
+                pass_on(way, distance, kind, lambda copy: copy.wait_send())
+        for level in range(top + 1):
+            aside(level, kind, 2 * level + e % 2).wait_send()
 
 
 def with_kernel(modal_history, stress_modes):
@@ -357,7 +399,8 @@
             dma((2,)), dma((2,)),
             dma((2,)), dma((2,)),
             dma((1,)), dma((1,)),
-            dma((elems, 2)), dma((elems, 2)),
+            dma((2, 3, 2)), dma((2, 3, 2)),
+            dma((elems // 2, 2)), dma((elems // 2, 2)),
             dma((2,)), dma((2,)),
             dma((elems, 2)), dma((elems, 2)),
         ],

time: 26.5 us -> 27.7 us (1.045)
  Pallas kernels: 24.9 us -> 26.1 us
    pallas_call x1, Pallas kernels: 24.9 us -> 26.1 us  [with_kernel(): pl.pallas_call(functools.partial(fused, elems, modes, width), out_shape=j...]
where the time goes in v4:
time: 27.7 us; the launch traced here: 27.5 us
  Pallas kernels  26.1 us (94%)
  local copies, waits for them, and re-layouts  1.42 us (5%)
    pallas_call x1, Pallas kernels, with_kernel(): pl.pallas_call(functools.partial(fused, elems, modes, width), out_shape=j...  26.1 us
    unnamed x3, local copies, waits for them, and re-layouts  1.42 us

profile of v4, /device:TPU:0, one launch (start us, length us, event | category | flops | bytes accessed | tf_op | source)
XLA Modules:
  0.0 27.5 jit_solution(13082497059809783113)
XLA Ops:
  0.0 0.0 copy-start
  0.0 0.7 %copy-done = f32[128,48]{0,1:T(8,128)S(1)} copy-done((f32[128,48]{0,1:T(8,128)S(1)}, f32[128,48]{0,1:T(8,128)}, u32[]{:S(2)}) %copy-start) | copy-done | bytes 24600
  0.7 26.1 %shard_map.37 = f32[12,32,128]{2,1,0:T(8,128)S(1)} custom-call(f32[16,2,16,128]{3,2,1,0:T(8,128)} %bitcast.11, f32[2,24,128]{2,1,0:T(8,128)S(1)} %bitcast.10, f32[384,128]{1,0:T(8,128)} %constant.2.clone.table), custom_call_target="tpu_custom_call" | custom-call | tf_op jit(solution)/shard_map/pallas_call | solution.py:383
  26.8 0.7 %copy.6 = f32[12,2,2048]{2,1,0:T(2,128)} copy(f32[12,2,2048]{2,1,0:T(2,128)S(1)} %bitcast.9) | data formatting | bytes 393216
Async XLA Ops:
  0.0 0.7 %copy-start = (f32[128,48]{0,1:T(8,128)S(1)}, f32[128,48]{0,1:T(8,128)}, u32[]{:S(2)}) copy-start(f32[128,48]{0,1:T(8,128)} %param.4) | copy-start | bytes 73732

commit v5 on v3

--- a/solution.py
+++ b/solution.py
@@ -170,14 +170,12 @@
         )
 
     shape_sends = []
-    steps_z = [elems // 2] + [d for d in range(2, elems, 2) if d != elems // 2]
+    order = sorted(range(1, elems), key=lambda d: -min(d, elems - d))
 
     def send_shapes(kind):
-        for d in steps_z:
+        for d in order:
             shape_sends.append(shape_copy(d, e, kind, (e + d) % elems))
             shape_sends[-1].start()
-        shape_sends.append(shape_copy(1, e, kind, beside))
-        shape_sends[-1].start()
 
     fetch_shapes.wait()
     send_shapes(0)
@@ -208,22 +206,14 @@
         own[c].wait()
         split_history(x, c)
 
+    for c in range(chunks):
+        from_across[c].wait_recv()
+        split_history(1 - x, c)
+
     for kind in range(2):
-        for d in sorted(steps_z, key=lambda d: min(d, elems - d)):
+        for d in order:
             source = (e + elems - d) % elems
             shape_copy(d, source, kind, source).wait_recv()
-            copy = shape_copy(d + 1, source, kind, beside)
-            copy.start()
-            shape_sends.append(copy)
-
-    from_across[0].wait_recv()
-    split_history(1 - x, 0)
-
-    for kind in range(2):
-        shape_copy(1, beside, kind, beside).wait_recv()
-        for d in steps_z:
-            source = (beside + elems - d) % elems
-            shape_copy(d + 1, source, kind, beside).wait_recv()
     s_hi, s_lo = split(
         jnp.concatenate(
             [
@@ -236,12 +226,8 @@
     s_both = jnp.concatenate([s_hi, s_lo], axis=0)
     rows = s_hi.shape[0]
 
-    order = sorted(range(1, elems), key=lambda d: -min(d, elems - d))
     last_copies, part_copies = [], []
     for c in range(chunks):
-        if c:
-            from_across[c].wait_recv()
-            split_history(1 - x, c)
         h_hi = jnp.concatenate([h_his[c, h] for h in range(2)], axis=1)
         h_lo = jnp.concatenate([h_los[c, h] for h in range(2)], axis=1)
         both = nt(s_both, h_hi)
@@ -259,7 +245,8 @@
         )
         copy.start()
         part_copies.append(copy)
-        copy.wait_recv()
+    for c in range(chunks):
+        part_copies[c].wait_recv()
         whole = parts[c, core] + other_parts[c]
         outbox[c] = whole
         for d in order:

time: 26.5 us -> 24.4 us (0.921)
  Pallas kernels: 24.9 us -> 22.8 us
    pallas_call x1, Pallas kernels: 24.9 us -> 22.8 us  [with_kernel(): pl.pallas_call(functools.partial(fused, elems, modes, width), out_shape=j...]
where the time goes in v5:
time: 24.4 us; the launch traced here: 24.2 us
  Pallas kernels  22.8 us (93%)
  local copies, waits for them, and re-layouts  1.42 us (6%)
    pallas_call x1, Pallas kernels, with_kernel(): pl.pallas_call(functools.partial(fused, elems, modes, width), out_shape=j...  22.8 us
    unnamed x3, local copies, waits for them, and re-layouts  1.42 us

profile of v5, /device:TPU:0, one launch (start us, length us, event | category | flops | bytes accessed | tf_op | source)
XLA Modules:
  0.0 24.2 jit_solution(5884783735696811658)
XLA Ops:
  0.0 0.0 copy-start
  0.0 0.7 %copy-done = f32[128,48]{0,1:T(8,128)S(1)} copy-done((f32[128,48]{0,1:T(8,128)S(1)}, f32[128,48]{0,1:T(8,128)}, u32[]{:S(2)}) %copy-start) | copy-done | bytes 24600
  0.7 22.8 %shard_map.37 = f32[12,32,128]{2,1,0:T(8,128)S(1)} custom-call(f32[16,2,16,128]{3,2,1,0:T(8,128)} %bitcast.11, f32[2,24,128]{2,1,0:T(8,128)S(1)} %bitcast.10, f32[384,128]{1,0:T(8,128)} %constant.2.clone.table), custom_call_target="tpu_custom_call" | custom-call | tf_op jit(solution)/shard_map/pallas_call | solution.py:328
  23.6 0.7 %copy.6 = f32[12,2,2048]{2,1,0:T(2,128)} copy(f32[12,2,2048]{2,1,0:T(2,128)S(1)} %bitcast.9) | data formatting | bytes 393216
Async XLA Ops:
  0.0 0.7 %copy-start = (f32[128,48]{0,1:T(8,128)S(1)}, f32[128,48]{0,1:T(8,128)}, u32[]{:S(2)}) copy-start(f32[128,48]{0,1:T(8,128)} %param.4) | copy-start | bytes 73732

commit v6 on v5

--- a/solution.py
+++ b/solution.py
@@ -129,6 +129,8 @@
     across = (m + 2) % modes
     beside = e + 1 - 2 * (e % 2)
     halves = (x, 1 - x)
+    ahead = [(e + d) % elems for d in range(elems)]
+    behind = [(e + elems - d) % elems for d in range(elems)]
 
     fetch_shapes = pltpu.make_async_copy(
         shapes.at[x], gathered.at[e, x], fetch_sem.at[0]
@@ -146,7 +148,7 @@
     barrier = pltpu.get_barrier_semaphore()
     for d in range(1, elems):
         pl.semaphore_signal(
-            barrier, inc=1, device_id=((e + d) % elems, m), device_id_type=MESH
+            barrier, inc=1, device_id=(ahead[d], m), device_id_type=MESH
         )
     for peer in (across, sibling):
         pl.semaphore_signal(barrier, inc=1, device_id=(e, peer), device_id_type=MESH)
@@ -165,7 +167,7 @@
     def shape_copy(slot, block, kind, peer):
         ref = gathered.at[block, halves[kind]]
         return pltpu.make_async_remote_copy(
-            ref, ref, s2s_sem.at[slot, kind], s2r_sem.at[slot, kind],
+            ref if kind else shapes.at[x], ref, s2s_sem.at[slot, kind], s2r_sem.at[slot, kind],
             device_id=(peer, m), device_id_type=MESH,
         )
 
@@ -174,10 +176,9 @@
 
     def send_shapes(kind):
         for d in order:
-            shape_sends.append(shape_copy(d, e, kind, (e + d) % elems))
+            shape_sends.append(shape_copy(d, e, kind, ahead[d]))
             shape_sends[-1].start()
 
-    fetch_shapes.wait()
     send_shapes(0)
 
     to_across, from_across = [
@@ -206,13 +207,17 @@
         own[c].wait()
         split_history(x, c)
 
-    for c in range(chunks):
-        from_across[c].wait_recv()
-        split_history(1 - x, c)
-
+    fetch_table.wait()
+    w_hi, w_lo = split(
+        jnp.concatenate([consts[:128, :], consts[128:256, :]], axis=1)
+    )
+    from_across[0].wait_recv()
+    split_history(1 - x, 0)
+
+    fetch_shapes.wait()
     for kind in range(2):
         for d in order:
-            source = (e + elems - d) % elems
+            source = behind[d]
             shape_copy(d, source, kind, source).wait_recv()
     s_hi, s_lo = split(
         jnp.concatenate(
@@ -228,6 +233,9 @@
 
     last_copies, part_copies = [], []
     for c in range(chunks):
+        if c:
+            from_across[c].wait_recv()
+            split_history(1 - x, c)
         h_hi = jnp.concatenate([h_his[c, h] for h in range(2)], axis=1)
         h_lo = jnp.concatenate([h_los[c, h] for h in range(2)], axis=1)
         both = nt(s_both, h_hi)
@@ -250,7 +258,7 @@
         whole = parts[c, core] + other_parts[c]
         outbox[c] = whole
         for d in order:
-            peer, source = (e + d) % elems, (e + elems - d) % elems
+            peer, source = ahead[d], behind[d]
             copy = pltpu.make_async_remote_copy(
                 outbox.at[c, peer], inbox.at[c, e], as_sem.at[d, c], ar_sem.at[d, c],
                 device_id=(peer, m), device_id_type=MESH,
@@ -263,10 +271,6 @@
             last_copies.append((c, copy, landed))
         inbox[c, e] = outbox[c, e]
 
-    fetch_table.wait()
-    w_hi, w_lo = split(
-        jnp.concatenate([consts[:128, :], consts[128:256, :]], axis=1)
-    )
     half = REST // 2
     total = None
     for c in range(chunks):
@@ -349,9 +353,9 @@
             dma((elems, 2)), dma((elems, 2)),
         ],
         compiler_params=pltpu.CompilerParams(
-            collective_id=0, has_side_effects=True, vmem_limit_bytes=55000 * 1024
+            collective_id=0, has_side_effects=True, vmem_limit_bytes=32 * 1024 * 1024
         ),
-    )(hist, shapes, table)
+    )(*[pltpu.with_memory_space_constraint(a, pltpu.HBM) for a in (hist, shapes, table)])
     ordered = result.reshape(width, REST // 2, 2, RADIX).transpose(0, 2, 1, 3)
     return ordered.reshape(width, 2, REST // 2 * RADIX)
 

time: 24.4 us -> 24 us (0.984)
  local copies, waits for them, and re-layouts: 1.42 us -> 0.68 us
  Pallas kernels: 22.8 us -> 23.1 us
    unnamed x3 -> x1, local copies, waits for them, and re-layouts: 1.42 us -> 0.68 us
    pallas_call x1, Pallas kernels: 22.8 us -> 23.1 us  [with_kernel(): pl.pallas_call(functools.partial(fused, elems, modes, width), out_shape=j...]
where the time goes in v6:
time: 24 us; the launch traced here: 23.8 us
  Pallas kernels  23.1 us (96%)
  local copies, waits for them, and re-layouts  0.68 us (3%)
    pallas_call x1, Pallas kernels, with_kernel(): pl.pallas_call(functools.partial(fused, elems, modes, width), out_shape=j...  23.1 us
    unnamed x1, local copies, waits for them, and re-layouts  0.68 us

profile of v6, /device:TPU:0, one launch (start us, length us, event | category | flops | bytes accessed | tf_op | source)
XLA Modules:
  0.0 23.8 jit_solution(4467023244879484914)
XLA Ops:
  0.0 23.1 %shard_map.37 = f32[12,32,128]{2,1,0:T(8,128)S(1)} custom-call(f32[16,2,16,128]{3,2,1,0:T(8,128)} %bitcast.10, f32[2,24,128]{2,1,0:T(8,128)} %bitcast.11, f32[384,128]{1,0:T(8,128)} %constant.2.clone.table), custom_call_target="tpu_custom_call" | custom-call | tf_op jit(solution)/shard_map/pallas_call | solution.py:332
  23.1 0.7 %copy.6 = f32[12,2,2048]{2,1,0:T(2,128)} copy(f32[12,2,2048]{2,1,0:T(2,128)S(1)} %bitcast.9) | data formatting | bytes 393216

commit v7 on v6

--- a/solution.py
+++ b/solution.py
@@ -102,12 +102,6 @@
     return hi, lo
 
 
-def nt(a, b):
-    return lax.dot_general(
-        a, b, (((1,), (1,)), ((), ())), preferred_element_type=f32
-    )
-
-
 def nn(a, b):
     return jnp.dot(a, b, preferred_element_type=f32)
 
@@ -118,7 +112,7 @@
     out,
     hbuf, h_his, h_los, gathered, parts, other_parts, outbox, inbox,
     turned, consts,
-    own_sem, fetch_sem, hs_sem, hr_sem, s1s_sem, s1r_sem, s2s_sem, s2r_sem,
+    own_sem, fetch_sem, hs_sem, hr_sem, s2s_sem, s2r_sem,
     ps_sem, pr_sem, as_sem, ar_sem,
 ):
     chunks = 2
@@ -145,41 +139,13 @@
         copy.start()
     fetch_table.start()
 
+    order = sorted(range(1, elems), key=lambda d: -min(d, elems - d))
     barrier = pltpu.get_barrier_semaphore()
-    for d in range(1, elems):
-        pl.semaphore_signal(
-            barrier, inc=1, device_id=(ahead[d], m), device_id_type=MESH
-        )
-    for peer in (across, sibling):
-        pl.semaphore_signal(barrier, inc=1, device_id=(e, peer), device_id_type=MESH)
-    pl.semaphore_wait(barrier, elems - 1 + 2)
-
-    to_regroup = pltpu.make_async_remote_copy(
-        shapes.at[1 - x], gathered.at[e, x], s1s_sem.at[0], s1r_sem.at[0],
-        device_id=(e, across), device_id_type=MESH,
-    )
-    from_regroup = pltpu.make_async_remote_copy(
-        shapes.at[1 - x], gathered.at[e, 1 - x], s1s_sem.at[0], s1r_sem.at[0],
-        device_id=(e, across), device_id_type=MESH,
-    )
-    to_regroup.start()
-
-    def shape_copy(slot, block, kind, peer):
-        ref = gathered.at[block, halves[kind]]
-        return pltpu.make_async_remote_copy(
-            ref if kind else shapes.at[x], ref, s2s_sem.at[slot, kind], s2r_sem.at[slot, kind],
-            device_id=(peer, m), device_id_type=MESH,
-        )
-
-    shape_sends = []
-    order = sorted(range(1, elems), key=lambda d: -min(d, elems - d))
-
-    def send_shapes(kind):
-        for d in order:
-            shape_sends.append(shape_copy(d, e, kind, ahead[d]))
-            shape_sends[-1].start()
-
-    send_shapes(0)
+    greeted = [(ahead[d], peer) for d in order for peer in (across, m)]
+    greeted += [(e, across), (e, sibling)]
+    for device in greeted:
+        pl.semaphore_signal(barrier, inc=1, device_id=device, device_id_type=MESH)
+    pl.semaphore_wait(barrier, len(greeted))
 
     to_across, from_across = [
         [
@@ -191,18 +157,37 @@
         ]
         for origin in (x, 1 - x)
     ]
-    for copy in to_across:
-        copy.start()
+    to_across[0].start()
+
+    shape_sends, shape_lands = [], []
+    for d in order + [0]:
+        for kind, side in ((0, m), (1, across)):
+            if d == 0 and kind == 0:
+                continue
+            source = behind[d]
+            send = pltpu.make_async_remote_copy(
+                shapes.at[halves[kind]], gathered.at[e, x],
+                s2s_sem.at[d, kind], s2r_sem.at[d, kind],
+                device_id=(ahead[d], side), device_id_type=MESH,
+            )
+            land = pltpu.make_async_remote_copy(
+                shapes.at[halves[kind]], gathered.at[source, halves[kind]],
+                s2s_sem.at[d, kind], s2r_sem.at[d, kind],
+                device_id=(source, side), device_id_type=MESH,
+            )
+            send.start()
+            shape_sends.append(send)
+            shape_lands.append(land)
+
+    to_across[1].start()
 
     def split_history(origin, c):
         flat = hbuf.at[origin, c].reshape(256, 128)
         turned_rows = [flat[pl.ds(i, 16, stride=16), :] for i in range(16)]
-        hi, lo = split(jnp.concatenate(turned_rows, axis=0))
+        hi, lo = split(jnp.concatenate(turned_rows, axis=0).T)
         h_his[c, origin] = hi
         h_los[c, origin] = lo
 
-    from_regroup.wait_recv()
-    send_shapes(1)
     for c in range(chunks):
         own[c].wait()
         split_history(x, c)
@@ -215,10 +200,8 @@
     split_history(1 - x, 0)
 
     fetch_shapes.wait()
-    for kind in range(2):
-        for d in order:
-            source = behind[d]
-            shape_copy(d, source, kind, source).wait_recv()
+    for land in shape_lands:
+        land.wait_recv()
     s_hi, s_lo = split(
         jnp.concatenate(
             [
@@ -236,10 +219,10 @@
         if c:
             from_across[c].wait_recv()
             split_history(1 - x, c)
-        h_hi = jnp.concatenate([h_his[c, h] for h in range(2)], axis=1)
-        h_lo = jnp.concatenate([h_los[c, h] for h in range(2)], axis=1)
-        both = nt(s_both, h_hi)
-        stress = both[:rows] + (both[rows:] + nt(s_hi, h_lo))
+        h_hi = jnp.concatenate([h_his[c, h] for h in range(2)], axis=0)
+        h_lo = jnp.concatenate([h_los[c, h] for h in range(2)], axis=0)
+        both = nn(s_both, h_hi)
+        stress = both[:rows] + (both[rows:] + nn(s_hi, h_lo))
         for owner in range(elems):
             for k in range(2):
                 for h in range(2):
@@ -316,7 +299,7 @@
 
     for _, copy, _ in last_copies:
         copy.wait_send()
-    for copy in [to_regroup] + shape_sends + to_across + part_copies:
+    for copy in shape_sends + to_across + part_copies:
         copy.wait_send()
 
 
@@ -336,8 +319,8 @@
         out_specs=pl.BlockSpec(memory_space=pltpu.VMEM),
         scratch_shapes=[
             pltpu.VMEM((2, 2, 16, 16, 128), f32),
-            pltpu.VMEM((2, 2, 256, 128), bf16),
-            pltpu.VMEM((2, 2, 256, 128), bf16),
+            pltpu.VMEM((2, 2, 128, 256), bf16),
+            pltpu.VMEM((2, 2, 128, 256), bf16),
             pltpu.VMEM((elems, 2, 2 * width, 128), f32),
             pltpu.VMEM((2, 2, elems, 2 * width, 128), f32),
             pltpu.VMEM((2, elems, 2 * width, 128), f32),
@@ -347,7 +330,6 @@
             pltpu.VMEM(table.shape, f32),
             dma((2,)), dma((2,)),
             dma((2,)), dma((2,)),
-            dma((1,)), dma((1,)),
             dma((elems, 2)), dma((elems, 2)),
             dma((2,)), dma((2,)),
             dma((elems, 2)), dma((elems, 2)),

time: 24 us -> 24 us (level)
  no operation moved by 1% of the time
where the time goes in v7:
time: 24 us; the launch traced here: 23.9 us
  Pallas kernels  23.2 us (97%)
  local copies, waits for them, and re-layouts  0.68 us (3%)
    pallas_call x1, Pallas kernels, with_kernel(): pl.pallas_call(functools.partial(fused, elems, modes, width), out_shape=j...  23.2 us
    unnamed x1, local copies, waits for them, and re-layouts  0.68 us

profile of v7, /device:TPU:0, one launch (start us, length us, event | category | flops | bytes accessed | tf_op | source)
XLA Modules:
  0.0 23.9 jit_solution(13284834964160502910)
XLA Ops:
  0.0 23.2 %shard_map.37 = f32[12,32,128]{2,1,0:T(8,128)S(1)} custom-call(f32[16,2,16,128]{3,2,1,0:T(8,128)} %bitcast.10, f32[2,24,128]{2,1,0:T(8,128)} %bitcast.11, f32[384,128]{1,0:T(8,128)} %constant.2.clone.table), custom_call_target="tpu_custom_call" | custom-call | tf_op jit(solution)/shard_map/pallas_call | solution.py:315
  23.2 0.7 %copy.6 = f32[12,2,2048]{2,1,0:T(2,128)} copy(f32[12,2,2048]{2,1,0:T(2,128)S(1)} %bitcast.9) | data formatting | bytes 393216

commit v8 on v6

--- a/solution.py
+++ b/solution.py
@@ -102,12 +102,6 @@
     return hi, lo
 
 
-def nt(a, b):
-    return lax.dot_general(
-        a, b, (((1,), (1,)), ((), ())), preferred_element_type=f32
-    )
-
-
 def nn(a, b):
     return jnp.dot(a, b, preferred_element_type=f32)
 
@@ -116,7 +110,7 @@
     elems, modes, width,
     hist, shapes, table,
     out,
-    hbuf, h_his, h_los, gathered, parts, other_parts, outbox, inbox,
+    hbuf, h_his, h_los, mine, gathered, parts, other_parts, outbox, inbox,
     turned, consts,
     own_sem, fetch_sem, hs_sem, hr_sem, s1s_sem, s1r_sem, s2s_sem, s2r_sem,
     ps_sem, pr_sem, as_sem, ar_sem,
@@ -133,7 +127,7 @@
     behind = [(e + elems - d) % elems for d in range(elems)]
 
     fetch_shapes = pltpu.make_async_copy(
-        shapes.at[x], gathered.at[e, x], fetch_sem.at[0]
+        shapes, mine, fetch_sem.at[0]
     )
     fetch_table = pltpu.make_async_copy(table, consts, fetch_sem.at[1])
     own = [
@@ -155,56 +149,58 @@
     pl.semaphore_wait(barrier, elems - 1 + 2)
 
     to_regroup = pltpu.make_async_remote_copy(
-        shapes.at[1 - x], gathered.at[e, x], s1s_sem.at[0], s1r_sem.at[0],
+        mine.at[1 - x], gathered.at[e, x], s1s_sem.at[0], s1r_sem.at[0],
         device_id=(e, across), device_id_type=MESH,
     )
     from_regroup = pltpu.make_async_remote_copy(
-        shapes.at[1 - x], gathered.at[e, 1 - x], s1s_sem.at[0], s1r_sem.at[0],
+        mine.at[1 - x], gathered.at[e, 1 - x], s1s_sem.at[0], s1r_sem.at[0],
         device_id=(e, across), device_id_type=MESH,
     )
+    fetch_shapes.wait()
     to_regroup.start()
-
-    def shape_copy(slot, block, kind, peer):
-        ref = gathered.at[block, halves[kind]]
-        return pltpu.make_async_remote_copy(
-            ref if kind else shapes.at[x], ref, s2s_sem.at[slot, kind], s2r_sem.at[slot, kind],
-            device_id=(peer, m), device_id_type=MESH,
-        )
-
-    shape_sends = []
-    order = sorted(range(1, elems), key=lambda d: -min(d, elems - d))
-
-    def send_shapes(kind):
-        for d in order:
-            shape_sends.append(shape_copy(d, e, kind, ahead[d]))
-            shape_sends[-1].start()
-
-    send_shapes(0)
 
     to_across, from_across = [
         [
             pltpu.make_async_remote_copy(
-                hist.at[:, c], hbuf.at[origin, c], hs_sem.at[c], hr_sem.at[c],
+                hbuf.at[x, c], hbuf.at[origin, c], hs_sem.at[c], hr_sem.at[c],
                 device_id=(e, across), device_id_type=MESH,
             )
             for c in range(chunks)
         ]
         for origin in (x, 1 - x)
     ]
-    for copy in to_across:
-        copy.start()
+    for c in range(chunks):
+        own[c].wait()
+        to_across[c].start()
+
+    def shape_copy(slot, block, kind, peer):
+        ref = gathered.at[block, halves[kind]]
+        return pltpu.make_async_remote_copy(
+            ref if kind else mine.at[x], ref, s2s_sem.at[slot, kind], s2r_sem.at[slot, kind],
+            device_id=(peer, m), device_id_type=MESH,
+        )
+
+    shape_sends = []
+    order = sorted(range(1, elems), key=lambda d: -min(d, elems - d))
+
+    def send_shapes(kind):
+        for d in order:
+            shape_sends.append(shape_copy(d, e, kind, ahead[d]))
+            shape_sends[-1].start()
+
+    send_shapes(0)
+    gathered[e, x] = mine[x]
 
     def split_history(origin, c):
         flat = hbuf.at[origin, c].reshape(256, 128)
         turned_rows = [flat[pl.ds(i, 16, stride=16), :] for i in range(16)]
-        hi, lo = split(jnp.concatenate(turned_rows, axis=0))
+        hi, lo = split(jnp.concatenate(turned_rows, axis=0).T)
         h_his[c, origin] = hi
         h_los[c, origin] = lo
 
     from_regroup.wait_recv()
     send_shapes(1)
     for c in range(chunks):
-        own[c].wait()
         split_history(x, c)
 
     fetch_table.wait()
@@ -214,7 +210,6 @@
     from_across[0].wait_recv()
     split_history(1 - x, 0)
 
-    fetch_shapes.wait()
     for kind in range(2):
         for d in order:
             source = behind[d]
@@ -236,10 +231,10 @@
         if c:
             from_across[c].wait_recv()
             split_history(1 - x, c)
-        h_hi = jnp.concatenate([h_his[c, h] for h in range(2)], axis=1)
-        h_lo = jnp.concatenate([h_los[c, h] for h in range(2)], axis=1)
-        both = nt(s_both, h_hi)
-        stress = both[:rows] + (both[rows:] + nt(s_hi, h_lo))
+        h_hi = jnp.concatenate([h_his[c, h] for h in range(2)], axis=0)
+        h_lo = jnp.concatenate([h_los[c, h] for h in range(2)], axis=0)
+        both = nn(s_both, h_hi)
+        stress = both[:rows] + (both[rows:] + nn(s_hi, h_lo))
         for owner in range(elems):
             for k in range(2):
                 for h in range(2):
@@ -336,8 +331,9 @@
         out_specs=pl.BlockSpec(memory_space=pltpu.VMEM),
         scratch_shapes=[
             pltpu.VMEM((2, 2, 16, 16, 128), f32),
-            pltpu.VMEM((2, 2, 256, 128), bf16),
-            pltpu.VMEM((2, 2, 256, 128), bf16),
+            pltpu.VMEM((2, 2, 128, 256), bf16),
+            pltpu.VMEM((2, 2, 128, 256), bf16),
+            pltpu.VMEM((2, 2 * width, 128), f32),
             pltpu.VMEM((elems, 2, 2 * width, 128), f32),
             pltpu.VMEM((2, 2, elems, 2 * width, 128), f32),
             pltpu.VMEM((2, elems, 2 * width, 128), f32),

time: 24 us -> 23.8 us (level)
  no operation moved by 1% of the time
where the time goes in v8:
time: 23.8 us; the launch traced here: 23.6 us
  Pallas kernels  22.9 us (96%)
  local copies, waits for them, and re-layouts  0.68 us (3%)
    pallas_call x1, Pallas kernels, with_kernel(): pl.pallas_call(functools.partial(fused, elems, modes, width), out_shape=j...  22.9 us
    unnamed x1, local copies, waits for them, and re-layouts  0.68 us

profile of v8, /device:TPU:0, one launch (start us, length us, event | category | flops | bytes accessed | tf_op | source)
XLA Modules:
  0.0 23.6 jit_solution(11320637077311398038)
XLA Ops:
  0.0 22.9 %shard_map.37 = f32[12,32,128]{2,1,0:T(8,128)S(1)} custom-call(f32[16,2,16,128]{3,2,1,0:T(8,128)} %bitcast.10, f32[2,24,128]{2,1,0:T(8,128)} %bitcast.11, f32[384,128]{1,0:T(8,128)} %constant.2.clone.table), custom_call_target="tpu_custom_call" | custom-call | tf_op jit(solution)/shard_map/pallas_call | solution.py:327
  23.0 0.7 %copy.6 = f32[12,2,2048]{2,1,0:T(2,128)} copy(f32[12,2,2048]{2,1,0:T(2,128)S(1)} %bitcast.9) | data formatting | bytes 393216

commit v9 on v8

--- a/solution.py
+++ b/solution.py
@@ -121,10 +121,12 @@
     x, core = m // 2, m % 2
     sibling = m + 1 - 2 * core
     across = (m + 2) % modes
-    beside = e + 1 - 2 * (e % 2)
     halves = (x, 1 - x)
-    ahead = [(e + d) % elems for d in range(elems)]
-    behind = [(e + elems - d) % elems for d in range(elems)]
+    flips = [1 - 2 * (e % 2), 2 - 4 * (e // 2 % 2), 4 - 8 * (e // 4)]
+    partner = [
+        e + sum(flips[i] for i in range(3) if d // 2**i % 2) for d in range(elems)
+    ]
+    order = range(elems - 1, 0, -1)
 
     fetch_shapes = pltpu.make_async_copy(
         shapes, mine, fetch_sem.at[0]
@@ -140,9 +142,9 @@
     fetch_table.start()
 
     barrier = pltpu.get_barrier_semaphore()
-    for d in range(1, elems):
+    for d in order:
         pl.semaphore_signal(
-            barrier, inc=1, device_id=(ahead[d], m), device_id_type=MESH
+            barrier, inc=1, device_id=(partner[d], m), device_id_type=MESH
         )
     for peer in (across, sibling):
         pl.semaphore_signal(barrier, inc=1, device_id=(e, peer), device_id_type=MESH)
@@ -181,11 +183,10 @@
         )
 
     shape_sends = []
-    order = sorted(range(1, elems), key=lambda d: -min(d, elems - d))
 
     def send_shapes(kind):
         for d in order:
-            shape_sends.append(shape_copy(d, e, kind, ahead[d]))
+            shape_sends.append(shape_copy(d, e, kind, partner[d]))
             shape_sends[-1].start()
 
     send_shapes(0)
@@ -212,7 +213,7 @@
 
     for kind in range(2):
         for d in order:
-            source = behind[d]
+            source = partner[d]
             shape_copy(d, source, kind, source).wait_recv()
     s_hi, s_lo = split(
         jnp.concatenate(
@@ -253,7 +254,7 @@
         whole = parts[c, core] + other_parts[c]
         outbox[c] = whole
         for d in order:
-            peer, source = ahead[d], behind[d]
+            peer, source = partner[d], partner[d]
             copy = pltpu.make_async_remote_copy(
                 outbox.at[c, peer], inbox.at[c, e], as_sem.at[d, c], ar_sem.at[d, c],
                 device_id=(peer, m), device_id_type=MESH,

time: 23.8 us -> 23.3 us (0.979)
  Pallas kernels: 22.9 us -> 22.4 us
    pallas_call x1, Pallas kernels: 22.9 us -> 22.4 us  [with_kernel(): pl.pallas_call(functools.partial(fused, elems, modes, width), out_shape=j...]
where the time goes in v9:
time: 23.3 us; the launch traced here: 23.1 us
  Pallas kernels  22.4 us (96%)
  local copies, waits for them, and re-layouts  0.68 us (3%)
    pallas_call x1, Pallas kernels, with_kernel(): pl.pallas_call(functools.partial(fused, elems, modes, width), out_shape=j...  22.4 us
    unnamed x1, local copies, waits for them, and re-layouts  0.68 us

profile of v9, /device:TPU:0, one launch (start us, length us, event | category | flops | bytes accessed | tf_op | source)
XLA Modules:
  0.0 23.1 jit_solution(8441112947007008748)
XLA Ops:
  0.0 22.4 %shard_map.37 = f32[12,32,128]{2,1,0:T(8,128)S(1)} custom-call(f32[16,2,16,128]{3,2,1,0:T(8,128)} %bitcast.10, f32[2,24,128]{2,1,0:T(8,128)} %bitcast.11, f32[384,128]{1,0:T(8,128)} %constant.2.clone.table), custom_call_target="tpu_custom_call" | custom-call | tf_op jit(solution)/shard_map/pallas_call | solution.py:328
  22.5 0.7 %copy.6 = f32[12,2,2048]{2,1,0:T(2,128)} copy(f32[12,2,2048]{2,1,0:T(2,128)S(1)} %bitcast.9) | data formatting | bytes 393216
